TPU v7x, 1024 devices: a whole 8x8x8 slice. The times are simulated.
1024 devices in a mesh: dp: 32 (over x, y_hi), tensor: 32 (over z, y_lo, core).
Axes of the slice: x: 8, y: 8 (y_hi: 4, y_lo: 2; y = y_hi * 2 + y_lo), z: 8, core: 2. Of those that a mesh axis runs over, the one named last changes fastest.
Arguments:
- tokens: bfloat16 [512, 18432], P('tensor', 'dp'), may hold values from -6 to 6
- up_weight: bfloat16 [18432, 36864], P('dp', 'tensor'), may hold values from -0.078125 to 0.078125
- down_weight: bfloat16 [36864, 18432], P('tensor', 'dp'), may hold values from -0.078125 to 0.078125
- keep_bits: int32 [512, 18432], P('tensor', 'dp'), may hold values 0 or 1
- prior_scale: float32 [1], replicated, may hold values from 60 to 200
Outputs:
- scaled: bfloat16 [512, 18432], P('tensor', 'dp')
- amax: float32 [1], replicated
All inputs are finite; a program needn't handle non-finite values. No bound on the sum of `keep_bits` on one device may be relied on, other than what follows from the above.
Results may differ from a plain program's by a relative error of at most 0.0045.
Values may be sent and summed in bfloat16 or wider, within the bound.
No kernel may reach another device: no remote copies, remote signals or barrier semaphores. Data moves between devices by JAX's collectives and lax.ppermute only.
A program may use at most 32 MiB of HBM per device.

v0:
```python
import jax
import jax.numpy as jnp
from jax import lax
from jax.sharding import PartitionSpec as P


def body(tokens, up_weight, down_weight, keep_bits, prior_scale):
    gathered = lax.all_gather(tokens, "tensor", axis=0, tiled=True)
    hidden = lax.psum_scatter(
        jnp.dot(gathered, up_weight, preferred_element_type=jnp.float32),
        "dp",
        scatter_dimension=0,
        tiled=True,
    )
    positive = jnp.maximum(hidden, 0.0)
    active = (positive * positive).astype(jnp.bfloat16)
    partial_out = jnp.dot(
        lax.all_gather(active, "dp", axis=0, tiled=True),
        down_weight,
        preferred_element_type=jnp.float32,
    )
    mlp_out = lax.psum_scatter(partial_out, "tensor", scatter_dimension=0, tiled=True)
    combined = tokens.astype(jnp.float32) + keep_bits.astype(jnp.float32) * mlp_out / 0.9
    local_max = jnp.max(jnp.abs(combined)).reshape(1)
    amax = lax.pmax(local_max, ("dp", "tensor"))
    scaled = jnp.clip(combined * prior_scale[0], -448.0, 448.0).astype(jnp.bfloat16)
    return (scaled, amax)


def solution(mesh):
    return jax.shard_map(
        body,
        mesh=mesh,
        in_specs=(P("tensor", "dp"), P("dp", "tensor"), P("tensor", "dp"), P("tensor", "dp"), P()),
        out_specs=(P("tensor", "dp"), P()),
        check_vma=False,
    )
```

profile of v0, /device:TPU:1, one launch (start us, length us, event | category | flops | bytes accessed | tf_op | source)
XLA Modules:
  0.0 630.8 jit_solution(8386263843816260577)
XLA Ops:
  7.2 0.0 copy-start
  7.2 0.0 reduce-scatter.3.cloned.1.call-start
  7.2 51.2 %all_gather.6 = bf16[512,576]{1,0:T(8,128)(2,1)S(1)} all-gather(bf16[16,576]{1,0:T(8,128)(2,1)} %param.5), channel_id=1, replica_groups=mesh['dp'=32,'tensor'=32] {'tensor'}, dimensions={0}, use_global_device_ids=true | all-gather | bytes 608256 | tf_op jit(solution)/shard_map/all_gather | solution.py:8
  58.4 0.0 copy-done
  58.4 2.6 fusion
  61.0 0.0 copy-start.3
  61.0 0.0 reduce-scatter.3.cloned.1.call-update
  61.0 0.0 all-gather.2.cloned.1.call-start
  61.1 226.3 %reduce-scatter.3.cloned.1.call-done = f32[16,1152]{1,0:T(8,128)} async-done(((f32[512,1152]{1,0:T(8,128)}), f32[16,1152]{1,0:T(8,128)}) %reduce-scatter.3.cloned.1.call-update) | async-done | bytes 73744 | tf_op jit(solution)/shard_map/reduce_scatter | solution.py:9
  287.4 1.5 multiply_convert_fusion
  288.9 0.0 all-gather.2.cloned.1.call-update
  289.0 0.0 reduce-scatter.5.cloned.1.call-start
  289.0 91.6 %all-gather.2.cloned.1.call-done = bf16[512,1152]{1,0:T(8,128)(2,1)} async-done(((bf16[16,1152]{1,0:T(8,128)(2,1)}), bf16[512,1152]{1,0:T(8,128)(2,1)}) %all-gather.2.cloned.1.call-update) | async-done | bytes 1179664 | tf_op jit(solution)/shard_map/all_gather | solution.py:18
  380.6 0.0 copy-done.3
  380.7 3.5 fusion.1
  384.2 0.0 copy-start.1
  384.2 0.0 copy-start.2
  384.2 0.0 reduce-scatter.5.cloned.1.call-update
  384.9 122.6 %reduce-scatter.5.cloned.1.call-done = f32[16,576]{1,0:T(8,128)} async-done(((f32[512,576]{1,0:T(8,128)}), f32[16,576]{1,0:T(8,128)}) %reduce-scatter.5.cloned.1.call-update) | async-done | bytes 36880 | tf_op jit(solution)/shard_map/reduce_scatter | solution.py:22
  507.4 0.0 copy-done.1
  507.4 0.0 copy-done.2
  507.4 2.1 abs_reduce_fusion
  509.5 114.8 %pmax.7 = f32[1]{0:T(128)} all-reduce(f32[1]{0:T(128)} %bitcast.1), channel_id=1, replica_groups=mesh['dp'=32,'tensor'=32] {'dp','tensor'}, use_global_device_ids=true, to_apply=%region_3.0 | all-reduce | flops 1 | bytes 8 | tf_op jit(solution)/shard_map/pmax | solution.py:25
Async XLA Ops:
  7.2 51.3 %copy-start = (bf16[576,1152]{1,0:T(8,128)(2,1)S(1)}, bf16[576,1152]{1,0:T(8,128)(2,1)}, u32[]{:S(2)}) copy-start(bf16[576,1152]{1,0:T(8,128)(2,1)} %param.6) | copy-start | bytes 3981316
  7.2 280.3 %reduce-scatter.3.cloned.1.call-start = ((), (), s32[]{:S(2)}) async-start(), calls=%async_computation.2 | async-start | bytes 2433024 | tf_op jit(solution)/shard_map/reduce_scatter | solution.py:9
  61.0 319.6 %copy-start.3 = (bf16[1152,576]{0,1:T(8,128)(2,1)S(1)}, bf16[1152,576]{0,1:T(8,128)(2,1)}, u32[]{:S(2)}) copy-start(bf16[1152,576]{0,1:T(8,128)(2,1)} %param.7) | copy-start | bytes 3981316
  61.0 319.6 %all-gather.2.cloned.1.call-start = ((), (), s32[]{:S(2)}) async-start(), calls=%async_computation.3 | async-start | bytes 1216512 | tf_op jit(solution)/shard_map/all_gather | solution.py:18
  289.0 218.5 %reduce-scatter.5.cloned.1.call-start = ((), (), s32[]{:S(2)}) async-start(), calls=%async_computation.4 | async-start | bytes 1351680 | tf_op jit(solution)/shard_map/reduce_scatter | solution.py:22
  384.2 123.2 %copy-start.1 = (bf16[16,576]{1,0:T(8,128)(2,1)S(1)}, bf16[16,576]{1,0:T(8,128)(2,1)}, u32[]{:S(2)}) copy-start(bf16[16,576]{1,0:T(8,128)(2,1)} %param.5) | copy-start | bytes 55300
  384.2 123.2 %copy-start.2 = (s32[16,576]{1,0:T(8,128)S(1)}, s32[16,576]{1,0:T(8,128)}, u32[]{:S(2)}) copy-start(s32[16,576]{1,0:T(8,128)} %param.8) | copy-start | bytes 110596
Sparse Core Ops, SparseCore 0:
  61.2 226.2 reduce-scatter.2
  292.5 88.1 all-gather.1
  384.4 122.9 reduce-scatter.4
where the time goes:
time: 631 us
  waiting for transfers between devices  441 us (70%)
  blocking collectives  166 us (26%)
  between operations  14.4 us (2%)
    reduce_scatter x1, waiting for transfers between devices, body(): lax.psum_scatter(jnp.dot(gathered, up_weight, preferred_element_type=jnp....  226 us
    reduce_scatter x1, waiting for transfers between devices, body(): lax.psum_scatter(partial_out, 'tensor', scatter_dimension=0, tiled=True)  123 us
    pmax x1, blocking collectives, body(): amax = lax.pmax(local_max, ('dp', 'tensor'))  115 us
    all_gather x1, waiting for transfers between devices, body(): lax.all_gather(active, 'dp', axis=0, tiled=True)  91.6 us
    all_gather x1, blocking collectives, body(): gathered = lax.all_gather(tokens, 'tensor', axis=0, tiled=True)  51.2 us
  transfers between devices with their start and end apart: 3, of which 3 were waited for; matrix products, arithmetic and copies ran while one was open for 0% of the time, Pallas kernels for 0%

commit v1 on v0

v1 whole, which is shorter than its diff:
```python
import jax
import jax.numpy as jnp
from jax import lax
from jax.sharding import Mesh, PartitionSpec as P

DP = ("x", "yh")
TENSOR = ("z", "yl", "core")
LIFT = 128.0


def exchange(blocks, axes):
    return lax.all_to_all(blocks, axes, split_axis=0, concat_axis=0, tiled=True)


def gather(block, axes, n):
    spread = exchange(jnp.broadcast_to(block, (n,) + block.shape), axes)
    return spread.reshape((n * block.shape[0],) + block.shape[1:])


def max_over(value, axes, n):
    return jnp.max(exchange(jnp.full((n, 1, 128), value), axes))


def body(tokens, up_weight, down_weight, keep_bits, prior_scale):
    rows, width = tokens.shape
    shards = up_weight.shape[1]
    half = gather(tokens, ("z", "yl"), 16)
    gathered = lax.all_gather(half, "core", axis=0, tiled=True)
    hidden_part = jnp.dot(gathered, up_weight, preferred_element_type=jnp.float32)
    hidden_part = (hidden_part * LIFT).astype(jnp.float16).reshape(32, rows, shards)
    hidden = jnp.sum(exchange(hidden_part, DP).astype(jnp.float32), axis=0) * (1.0 / LIFT)
    positive = jnp.maximum(hidden, 0.0)
    active = gather((positive * positive).astype(jnp.bfloat16), DP, 32)
    out_part = jnp.dot(active, down_weight, preferred_element_type=jnp.float32)
    out_part = lax.psum_scatter(out_part, "core", scatter_dimension=0, tiled=True)
    out_part = out_part.astype(jnp.bfloat16).reshape(16, rows, width)
    mlp_out = jnp.sum(exchange(out_part, ("z", "yl")).astype(jnp.float32), axis=0)
    combined = tokens.astype(jnp.float32) + keep_bits.astype(jnp.float32) * mlp_out / 0.9
    amax = max_over(max_over(jnp.max(jnp.abs(combined)), DP, 32), TENSOR, 32).reshape(1)
    scaled = jnp.clip(combined * prior_scale[0], -448.0, 448.0).astype(jnp.bfloat16)
    return (scaled, amax)


def solution(mesh):
    fine = Mesh(mesh.devices.reshape(8, 4, 8, 2, 2), DP + TENSOR)
    return jax.shard_map(
        body,
        mesh=fine,
        in_specs=(P(TENSOR, DP), P(DP, TENSOR), P(TENSOR, DP), P(TENSOR, DP), P()),
        out_specs=(P(TENSOR, DP), P()),
        check_vma=False,
    )
```

time: 631 us -> 209 us (0.33)
  waiting for transfers between devices: 441 us -> 25.8 us
  blocking collectives: 166 us -> 151 us
  starting transfers between devices: 0.12 us -> 6.46 us
    reduce_scatter x2 -> x1, waiting for transfers between devices: 349 us -> 15.1 us  [body(): lax.psum_scatter(out_part, 'core', scatter_dimension=0, tiled=True)]
    all_to_all x0 -> x5, blocking collectives: none -> 147 us  [exchange(): return lax.all_to_all(blocks, axes, split_axis=0, concat_axis=0, tiled=True)]
    pmax x1 -> x0, blocking collectives: 115 us -> none  [body(): amax = lax.pmax(local_max, ('dp', 'tensor'))]
    all_gather x1 -> x0, waiting for transfers between devices: 91.6 us -> none  [body(): lax.all_gather(active, 'dp', axis=0, tiled=True)]
    all_gather x1, blocking collectives: 51.2 us -> 4.35 us  [body(): gathered = lax.all_gather(half, 'core', axis=0, tiled=True)]
    all_to_all x0 -> x1, waiting for transfers between devices: none -> 10.7 us  [exchange(): return lax.all_to_all(blocks, axes, split_axis=0, concat_axis=0, tiled=True)]
    all_to_all x0 -> x1, starting transfers between devices: none -> 6.42 us  [exchange(): return lax.all_to_all(blocks, axes, split_axis=0, concat_axis=0, tiled=True)]
  transfers between devices with their start and end apart: 3 -> 2, of which waited for: 3 -> 2; matrix products, arithmetic and copies ran while one was open for 0% -> 0% of each run, Pallas kernels for 0% -> 0%
where the time goes in v1:
time: 209 us
  blocking collectives  151 us (72%)
  waiting for transfers between devices  25.8 us (12%)
  between operations  14.8 us (7%)
  starting transfers between devices  6.46 us (3%)
  other arithmetic  3.84 us (2%)
  local copies, waits for them, and re-layouts  3.2 us (2%)
  matrix products  3.12 us (1%)
    all_to_all x5, blocking collectives, exchange(): return lax.all_to_all(blocks, axes, split_axis=0, concat_axis=0, tiled=True)  147 us
    reduce_scatter x1, waiting for transfers between devices, body(): lax.psum_scatter(out_part, 'core', scatter_dimension=0, tiled=True)  15.1 us
    all_to_all x1, waiting for transfers between devices, exchange(): return lax.all_to_all(blocks, axes, split_axis=0, concat_axis=0, tiled=True)  10.7 us
    all_to_all x1, starting transfers between devices, exchange(): return lax.all_to_all(blocks, axes, split_axis=0, concat_axis=0, tiled=True)  6.42 us
    all_gather x1, blocking collectives, body(): gathered = lax.all_gather(half, 'core', axis=0, tiled=True)  4.35 us
  transfers between devices with their start and end apart: 2, of which 2 were waited for; matrix products, arithmetic and copies ran while one was open for 0% of the time, Pallas kernels for 0%

profile of v1, /device:TPU:1, one launch (start us, length us, event | category | flops | bytes accessed | tf_op | source)
XLA Modules:
  0.0 208.6 jit_solution(15133355729412916549)
XLA Ops:
  7.2 0.0 copy-start
  7.2 0.0 reduce-scatter.2.cloned.1.call-start
  7.2 0.8 broadcast_in_dim.12
  8.1 29.5 %all_to_all.30 = bf16[16,16,576]{2,1,0:T(8,128)(2,1)S(1)} all-to-all(bf16[16,16,576]{2,1,0:T(8,128)(2,1)S(1)} %broadcast_in_dim.12), channel_id=1, replica_groups=mesh['x'=8,'yh'=4,'z'=8,'yl'=2,'core'=2] {'z','yl'}, dimensions={0} | all-to-all | bytes 589824 | tf_op jit(solution)/shard_map/all_to_all | solution.py:12
  37.5 4.3 %all_gather.3 = bf16[512,576]{1,0:T(8,128)(2,1)S(1)} all-gather(bf16[256,576]{1,0:T(8,128)(2,1)S(1)} %bitcast.13), channel_id=1, replica_groups=mesh['x'=8,'yh'=4,'z'=8,'yl'=2,'core'=2] {'core'}, dimensions={0}, use_global_device_ids=true | all-gather | bytes 884736 | tf_op jit(solution)/shard_map/all_gather | solution.py:28
  41.9 0.0 copy-done
  41.9 1.2 fusion
  43.1 44.7 %all_to_all.31 = f16[32,16,1152]{2,1,0:T(8,128)(2,1)S(1)} all-to-all(f16[32,16,1152]{2,1,0:T(8,128)(2,1)S(1)} %bitcast.14), channel_id=1, replica_groups=mesh['x'=8,'yh'=4,'z'=8,'yl'=2,'core'=2] {'x','yh'}, dimensions={0} | all-to-all | bytes 2359296 | tf_op jit(solution)/shard_map/all_to_all | solution.py:12
  87.8 0.2 convert_reduce_fusion
  88.0 0.1 broadcast_in_dim.13
  88.1 0.0 copy-start.3
  88.1 36.5 %all_to_all.32 = bf16[32,16,1152]{2,1,0:T(8,128)(2,1)S(1)} all-to-all(bf16[32,16,1152]{2,1,0:T(8,128)(2,1)S(1)} %broadcast_in_dim.13), channel_id=1, replica_groups=mesh['x'=8,'yh'=4,'z'=8,'yl'=2,'core'=2] {'x','yh'}, dimensions={0} | all-to-all | bytes 2359296 | tf_op jit(solution)/shard_map/all_to_all | solution.py:12
  124.5 0.0 copy-done.3
  124.5 2.0 fusion.1
  126.5 0.0 reduce-scatter.2.cloned.1.call-update
  126.5 0.0 copy-start.1
  126.5 0.0 copy-start.2
  126.6 15.1 %reduce-scatter.2.cloned.1.call-done = f32[256,576]{0,1:T(8,128)} async-done(((f32[512,576]{0,1:T(8,128)}), f32[256,576]{0,1:T(8,128)}) %reduce-scatter.2.cloned.1.call-update) | async-done | bytes 589840 | tf_op jit(solution)/shard_map/reduce_scatter | solution.py:35
  141.7 1.1 convert_element_type.29
  142.8 0.9 copy.9
  143.7 6.4 %all-to-all-start.3 = ((bf16[16,16,576]{2,1,0:T(8,128)(2,1)}), bf16[16,16,576]{2,1,0:T(8,128)(2,1)S(1)}, u32[]{:S(2)}, u32[]{:S(2)}) async-start(bf16[16,16,576]{2,1,0:T(8,128)(2,1)} %bitcast.3), calls=%async_computation.4 | async-start | bytes 655360 | tf_op jit(solution)/shard_map/all_to_all | solution.py:12
  150.8 10.7 %all-to-all-done.3 = bf16[16,16,576]{2,1,0:T(8,128)(2,1)S(1)} async-done(((bf16[16,16,576]{2,1,0:T(8,128)(2,1)}), bf16[16,16,576]{2,1,0:T(8,128)(2,1)S(1)}, u32[]{:S(2)}, u32[]{:S(2)}) %all-to-all-start.3) | async-done | bytes 294944 | tf_op jit(solution)/shard_map/all_to_all | solution.py:12
  161.4 0.1 convert_reduce_fusion.1
  161.5 0.0 copy-done.1
  161.5 0.0 copy-done.2
  161.5 1.3 abs_reduce_fusion
  162.8 0.7 broadcast_in_dim.14
  163.5 21.6 %all_to_all.33 = f32[32,1,128]{2,1,0:T(1,128)S(1)} all-to-all(f32[32,1,128]{2,1,0:T(1,128)S(1)} %broadcast_in_dim.14), channel_id=1, replica_groups=mesh['x'=8,'yh'=4,'z'=8,'yl'=2,'core'=2] {'x','yh'}, dimensions={0} | all-to-all | bytes 32768 | tf_op jit(solution)/shard_map/all_to_all | solution.py:12
  185.2 0.6 reduce_max.28
  185.8 0.7 broadcast_in_dim.15
  186.4 14.7 %all_to_all.34 = f32[32,1,128]{2,1,0:T(1,128)S(1)} all-to-all(f32[32,1,128]{2,1,0:T(1,128)S(1)} %broadcast_in_dim.15), channel_id=1, replica_groups=mesh['x'=8,'yh'=4,'z'=8,'yl'=2,'core'=2] {'z','yl','core'}, dimensions={0} | all-to-all | bytes 32768 | tf_op jit(solution)/shard_map/all_to_all | solution.py:12
  201.2 0.6 reduce_max.29
  (1 shorter events, 0.0 us)
Async XLA Ops:
  7.2 34.7 %copy-start = (bf16[576,1152]{1,0:T(8,128)(2,1)S(1)}, bf16[576,1152]{1,0:T(8,128)(2,1)}, u32[]{:S(2)}) copy-start(bf16[576,1152]{1,0:T(8,128)(2,1)} %param.6) | copy-start | bytes 3981316
  7.2 134.5 %reduce-scatter.2.cloned.1.call-start = ((), (), s32[]{:S(2)}) async-start(), calls=%async_computation.7 | async-start | bytes 1769472 | tf_op jit(solution)/shard_map/reduce_scatter | solution.py:35
  88.1 36.5 %copy-start.3 = (bf16[1152,576]{0,1:T(8,128)(2,1)S(1)}, bf16[1152,576]{0,1:T(8,128)(2,1)}, u32[]{:S(2)}) copy-start(bf16[1152,576]{0,1:T(8,128)(2,1)} %param.7) | copy-start | bytes 3981316
  126.5 35.0 %copy-start.1 = (bf16[16,576]{1,0:T(8,128)(2,1)S(1)}, bf16[16,576]{1,0:T(8,128)(2,1)}, u32[]{:S(2)}) copy-start(bf16[16,576]{1,0:T(8,128)(2,1)} %param.5) | copy-start | bytes 55300
  126.5 35.0 %copy-start.2 = (s32[16,576]{1,0:T(8,128)S(1)}, s32[16,576]{1,0:T(8,128)}, u32[]{:S(2)}) copy-start(s32[16,576]{1,0:T(8,128)} %param.8) | copy-start | bytes 110596
  143.7 17.8 %all-to-all-start.3 = ((bf16[16,16,576]{2,1,0:T(8,128)(2,1)}), bf16[16,16,576]{2,1,0:T(8,128)(2,1)S(1)}, u32[]{:S(2)}, u32[]{:S(2)}) async-start(bf16[16,16,576]{2,1,0:T(8,128)(2,1)} %bitcast.3), calls=%async_computation.4 | async-start | bytes 655360 | tf_op jit(solution)/shard_map/all_to_all | solution.py:12
Sparse Core Ops, SparseCore 0:
  126.7 14.9 reduce-scatter.1

commit v2 on v1

--- a/solution.py
+++ b/solution.py
@@ -1,11 +1,13 @@
 import jax
 import jax.numpy as jnp
 from jax import lax
+from jax.experimental.layout import Layout, with_layout_constraint
 from jax.sharding import Mesh, PartitionSpec as P
 
 DP = ("x", "yh")
 TENSOR = ("z", "yl", "core")
 LIFT = 128.0
+ROW_MAJOR = Layout(major_to_minor=(0, 1))
 
 
 def exchange(blocks, axes):
@@ -32,8 +34,9 @@
     positive = jnp.maximum(hidden, 0.0)
     active = gather((positive * positive).astype(jnp.bfloat16), DP, 32)
     out_part = jnp.dot(active, down_weight, preferred_element_type=jnp.float32)
-    out_part = lax.psum_scatter(out_part, "core", scatter_dimension=0, tiled=True)
-    out_part = out_part.astype(jnp.bfloat16).reshape(16, rows, width)
+    out_part = with_layout_constraint(out_part, ROW_MAJOR)
+    pair = exchange(out_part.reshape(2, 16, rows, width), "core")
+    out_part = (pair[0] + pair[1]).astype(jnp.bfloat16)
     mlp_out = jnp.sum(exchange(out_part, ("z", "yl")).astype(jnp.float32), axis=0)
     combined = tokens.astype(jnp.float32) + keep_bits.astype(jnp.float32) * mlp_out / 0.9
     amax = max_over(max_over(jnp.max(jnp.abs(combined)), DP, 32), TENSOR, 32).reshape(1)

time: 209 us -> 177 us (0.85)
  waiting for transfers between devices: 25.8 us -> 10.7 us
  between operations: 14.8 us -> 1.38 us
  starting transfers between devices: 6.46 us -> 3.54 us
    reduce_scatter x1 -> x0, waiting for transfers between devices: 15.1 us -> none  [body(): lax.psum_scatter(out_part, 'core', scatter_dimension=0, tiled=True)]
    all_to_all x1, starting transfers between devices: 6.42 us -> 3.54 us  [exchange(): return lax.all_to_all(blocks, axes, split_axis=0, concat_axis=0, tiled=True)]
    all_to_all x5 -> x6, blocking collectives: 147 us -> 149 us  [exchange(): return lax.all_to_all(blocks, axes, split_axis=0, concat_axis=0, tiled=True)]
  transfers between devices with their start and end apart: 2 -> 1, of which waited for: 2 -> 1; matrix products, arithmetic and copies ran while one was open for 0% -> 0% of each run, Pallas kernels for 0% -> 0%
where the time goes in v2:
time: 177 us
  blocking collectives  153 us (86%)
  waiting for transfers between devices  10.7 us (6%)
  starting transfers between devices  3.54 us (2%)
  other arithmetic  3.52 us (2%)
  matrix products  2.33 us (1%)
  local copies, waits for them, and re-layouts  2.32 us (1%)
    all_to_all x6, blocking collectives, exchange(): return lax.all_to_all(blocks, axes, split_axis=0, concat_axis=0, tiled=True)  149 us
    all_to_all x1, waiting for transfers between devices, exchange(): return lax.all_to_all(blocks, axes, split_axis=0, concat_axis=0, tiled=True)  10.7 us
    all_gather x1, blocking collectives, body(): gathered = lax.all_gather(half, 'core', axis=0, tiled=True)  4.35 us
    all_to_all x1, starting transfers between devices, exchange(): return lax.all_to_all(blocks, axes, split_axis=0, concat_axis=0, tiled=True)  3.54 us
  transfers between devices with their start and end apart: 1, of which 1 were waited for; matrix products, arithmetic and copies ran while one was open for 0% of the time, Pallas kernels for 0%

profile of v2, /device:TPU:1, one launch (start us, length us, event | category | flops | bytes accessed | tf_op | source)
XLA Modules:
  0.0 177.0 jit_solution(9440061641457402644)
XLA Ops:
  0.6 0.0 copy-start
  0.6 0.9 broadcast_in_dim.12
  1.5 29.5 %all_to_all.35 = bf16[16,16,576]{2,1,0:T(8,128)(2,1)S(1)} all-to-all(bf16[16,16,576]{2,1,0:T(8,128)(2,1)S(1)} %broadcast_in_dim.12), channel_id=1, replica_groups=mesh['x'=8,'yh'=4,'z'=8,'yl'=2,'core'=2] {'z','yl'}, dimensions={0} | all-to-all | bytes 589824 | tf_op jit(solution)/shard_map/all_to_all | solution.py:14
  31.0 4.3 %all_gather.3 = bf16[512,576]{1,0:T(8,128)(2,1)S(1)} all-gather(bf16[256,576]{1,0:T(8,128)(2,1)S(1)} %bitcast.16), channel_id=1, replica_groups=mesh['x'=8,'yh'=4,'z'=8,'yl'=2,'core'=2] {'core'}, dimensions={0}, use_global_device_ids=true | all-gather | bytes 884736 | tf_op jit(solution)/shard_map/all_gather | solution.py:30
  35.3 0.0 copy-done
  35.3 1.2 fusion
  36.5 44.7 %all_to_all.36 = f16[32,16,1152]{2,1,0:T(8,128)(2,1)S(1)} all-to-all(f16[32,16,1152]{2,1,0:T(8,128)(2,1)S(1)} %bitcast.17), channel_id=1, replica_groups=mesh['x'=8,'yh'=4,'z'=8,'yl'=2,'core'=2] {'x','yh'}, dimensions={0} | all-to-all | bytes 2359296 | tf_op jit(solution)/shard_map/all_to_all | solution.py:14
  81.2 0.2 convert_reduce_fusion
  81.4 0.1 broadcast_in_dim.13
  81.5 0.0 copy-start.3
  81.5 36.5 %all_to_all.37 = bf16[32,16,1152]{2,1,0:T(8,128)(2,1)S(1)} all-to-all(bf16[32,16,1152]{2,1,0:T(8,128)(2,1)S(1)} %broadcast_in_dim.13), channel_id=1, replica_groups=mesh['x'=8,'yh'=4,'z'=8,'yl'=2,'core'=2] {'x','yh'}, dimensions={0} | all-to-all | bytes 2359296 | tf_op jit(solution)/shard_map/all_to_all | solution.py:14
  118.0 0.0 copy-done.3
  118.0 1.2 fusion.3
  119.2 8.3 %all_to_all.38 = f32[2,16,16,576]{3,2,1,0:T(8,128)S(1)} all-to-all(f32[2,16,16,576]{3,2,1,0:T(8,128)S(1)} %bitcast.15), channel_id=1, replica_groups=mesh['x'=8,'yh'=4,'z'=8,'yl'=2,'core'=2] {'core'}, dimensions={0} | all-to-all | bytes 2359296 | tf_op jit(solution)/shard_map/all_to_all | solution.py:14
  127.5 0.0 copy-start.1
  127.5 0.0 copy-start.2
  127.5 0.8 fusion.2
  128.3 3.5 %all-to-all-start.4 = ((bf16[16,16,576]{2,1,0:T(8,128)(2,1)}), bf16[16,16,576]{2,1,0:T(8,128)(2,1)S(1)}, u32[]{:S(2)}, u32[]{:S(2)}) async-start(bf16[16,16,576]{2,1,0:T(8,128)(2,1)} %fusion.2), calls=%async_computation.4 | async-start | bytes 655360 | tf_op jit(solution)/shard_map/all_to_all | solution.py:14
  132.5 10.7 %all-to-all-done.4 = bf16[16,16,576]{2,1,0:T(8,128)(2,1)S(1)} async-done(((bf16[16,16,576]{2,1,0:T(8,128)(2,1)}), bf16[16,16,576]{2,1,0:T(8,128)(2,1)S(1)}, u32[]{:S(2)}, u32[]{:S(2)}) %all-to-all-start.4) | async-done | bytes 294944 | tf_op jit(solution)/shard_map/all_to_all | solution.py:14
  143.1 0.1 convert_reduce_fusion.1
  143.2 0.0 copy-done.1
  143.2 0.0 copy-done.2
  143.2 1.3 abs_reduce_fusion
  144.5 0.7 broadcast_in_dim.14
  145.2 15.4 %all_to_all.39 = f32[32,1,128]{2,1,0:T(1,128)S(1)} all-to-all(f32[32,1,128]{2,1,0:T(1,128)S(1)} %broadcast_in_dim.14), channel_id=1, replica_groups=mesh['x'=8,'yh'=4,'z'=8,'yl'=2,'core'=2] {'x','yh'}, dimensions={0} | all-to-all | bytes 32768 | tf_op jit(solution)/shard_map/all_to_all | solution.py:14
  160.6 0.6 reduce_max.28
  161.2 0.7 broadcast_in_dim.15
  161.9 14.5 %all_to_all.40 = f32[32,1,128]{2,1,0:T(1,128)S(1)} all-to-all(f32[32,1,128]{2,1,0:T(1,128)S(1)} %broadcast_in_dim.15), channel_id=1, replica_groups=mesh['x'=8,'yh'=4,'z'=8,'yl'=2,'core'=2] {'z','yl','core'}, dimensions={0} | all-to-all | bytes 32768 | tf_op jit(solution)/shard_map/all_to_all | solution.py:14
  176.4 0.6 reduce_max.29
  (1 shorter events, 0.0 us)
Async XLA Ops:
  0.6 34.7 %copy-start = (bf16[576,1152]{1,0:T(8,128)(2,1)S(1)}, bf16[576,1152]{1,0:T(8,128)(2,1)}, u32[]{:S(2)}) copy-start(bf16[576,1152]{1,0:T(8,128)(2,1)} %param.6) | copy-start | bytes 3981316
  81.5 36.6 %copy-start.3 = (bf16[1152,576]{0,1:T(8,128)(2,1)S(1)}, bf16[1152,576]{0,1:T(8,128)(2,1)}, u32[]{:S(2)}) copy-start(bf16[1152,576]{0,1:T(8,128)(2,1)} %param.7) | copy-start | bytes 3981316
  127.5 15.7 %copy-start.1 = (bf16[16,576]{1,0:T(8,128)(2,1)S(1)}, bf16[16,576]{1,0:T(8,128)(2,1)}, u32[]{:S(2)}) copy-start(bf16[16,576]{1,0:T(8,128)(2,1)} %param.5) | copy-start | bytes 55300
  127.5 15.7 %copy-start.2 = (s32[16,576]{1,0:T(8,128)S(1)}, s32[16,576]{1,0:T(8,128)}, u32[]{:S(2)}) copy-start(s32[16,576]{1,0:T(8,128)} %param.8) | copy-start | bytes 110596
  128.3 14.9 %all-to-all-start.4 = ((bf16[16,16,576]{2,1,0:T(8,128)(2,1)}), bf16[16,16,576]{2,1,0:T(8,128)(2,1)S(1)}, u32[]{:S(2)}, u32[]{:S(2)}) async-start(bf16[16,16,576]{2,1,0:T(8,128)(2,1)} %fusion.2), calls=%async_computation.4 | async-start | bytes 655360 | tf_op jit(solution)/shard_map/all_to_all | solution.py:14

commit v3 on v2

--- a/solution.py
+++ b/solution.py
@@ -19,8 +19,8 @@
     return spread.reshape((n * block.shape[0],) + block.shape[1:])
 
 
-def max_over(value, axes, n):
-    return jnp.max(exchange(jnp.full((n, 1, 128), value), axes))
+def max_over(values, axes, n):
+    return jnp.max(exchange(jnp.broadcast_to(values, (n,) + values.shape), axes), axis=0)
 
 
 def body(tokens, up_weight, down_weight, keep_bits, prior_scale):
@@ -30,16 +30,18 @@
     gathered = lax.all_gather(half, "core", axis=0, tiled=True)
     hidden_part = jnp.dot(gathered, up_weight, preferred_element_type=jnp.float32)
     hidden_part = (hidden_part * LIFT).astype(jnp.float16).reshape(32, rows, shards)
-    hidden = jnp.sum(exchange(hidden_part, DP).astype(jnp.float32), axis=0) * (1.0 / LIFT)
+    hidden = jnp.sum(exchange(hidden_part, ("yh", "x")).astype(jnp.float32), axis=0) * (1.0 / LIFT)
     positive = jnp.maximum(hidden, 0.0)
-    active = gather((positive * positive).astype(jnp.bfloat16), DP, 32)
+    active = gather((positive * positive).astype(jnp.bfloat16), "x", 8)
+    active = gather(active, "yh", 4)
     out_part = jnp.dot(active, down_weight, preferred_element_type=jnp.float32)
     out_part = with_layout_constraint(out_part, ROW_MAJOR)
     pair = exchange(out_part.reshape(2, 16, rows, width), "core")
     out_part = (pair[0] + pair[1]).astype(jnp.bfloat16)
     mlp_out = jnp.sum(exchange(out_part, ("z", "yl")).astype(jnp.float32), axis=0)
     combined = tokens.astype(jnp.float32) + keep_bits.astype(jnp.float32) * mlp_out / 0.9
-    amax = max_over(max_over(jnp.max(jnp.abs(combined)), DP, 32), TENSOR, 32).reshape(1)
+    largest = jnp.max(jnp.abs(combined), axis=0, keepdims=True)
+    amax = jnp.max(max_over(max_over(largest, DP, 32), TENSOR, 32)).reshape(1)
     scaled = jnp.clip(combined * prior_scale[0], -448.0, 448.0).astype(jnp.bfloat16)
     return (scaled, amax)
 

time: 177 us -> 185 us (1.045)
  blocking collectives: 153 us -> 160 us
  starting transfers between devices: 3.54 us -> 6.63 us
    all_to_all x6 -> x7, blocking collectives: 149 us -> 155 us  [exchange(): return lax.all_to_all(blocks, axes, split_axis=0, concat_axis=0, tiled=True)]
    all_to_all x1, starting transfers between devices: 3.54 us -> 6.63 us  [exchange(): return lax.all_to_all(blocks, axes, split_axis=0, concat_axis=0, tiled=True)]
where the time goes in v3:
time: 185 us; the launch traced here: 184 us
  blocking collectives  160 us (86%)
  waiting for transfers between devices  10.7 us (6%)
  starting transfers between devices  6.63 us (4%)
  other arithmetic  2.48 us (1%)
  matrix products  2.34 us (1%)
    all_to_all x7, blocking collectives, exchange(): return lax.all_to_all(blocks, axes, split_axis=0, concat_axis=0, tiled=True)  155 us
    all_to_all x1, waiting for transfers between devices, exchange(): return lax.all_to_all(blocks, axes, split_axis=0, concat_axis=0, tiled=True)  10.7 us
    all_to_all x1, starting transfers between devices, exchange(): return lax.all_to_all(blocks, axes, split_axis=0, concat_axis=0, tiled=True)  6.63 us
    all_gather x1, blocking collectives, body(): gathered = lax.all_gather(half, 'core', axis=0, tiled=True)  4.35 us
  transfers between devices with their start and end apart: 1, of which 1 were waited for; matrix products, arithmetic and copies ran while one was open for 0% of the time, Pallas kernels for 0%

profile of v3, /device:TPU:1, one launch (start us, length us, event | category | flops | bytes accessed | tf_op | source)
XLA Modules:
  0.0 184.1 jit_solution(10336348579538471350)
XLA Ops:
  0.6 0.0 copy-start
  0.6 0.9 broadcast_in_dim.16
  1.5 29.5 %all_to_all.40 = bf16[16,16,576]{2,1,0:T(8,128)(2,1)S(1)} all-to-all(bf16[16,16,576]{2,1,0:T(8,128)(2,1)S(1)} %broadcast_in_dim.16), channel_id=1, replica_groups=mesh['x'=8,'yh'=4,'z'=8,'yl'=2,'core'=2] {'z','yl'}, dimensions={0} | all-to-all | bytes 589824 | tf_op jit(solution)/shard_map/all_to_all | solution.py:14
  31.0 4.3 %all_gather.3 = bf16[512,576]{1,0:T(8,128)(2,1)S(1)} all-gather(bf16[256,576]{1,0:T(8,128)(2,1)S(1)} %bitcast.15), channel_id=1, replica_groups=mesh['x'=8,'yh'=4,'z'=8,'yl'=2,'core'=2] {'core'}, dimensions={0}, use_global_device_ids=true | all-gather | bytes 884736 | tf_op jit(solution)/shard_map/all_gather | solution.py:30
  35.3 0.0 copy-done
  35.3 1.2 fusion
  36.5 45.7 %all_to_all.41 = f16[32,16,1152]{2,1,0:T(8,128)(2,1)S(1)} all-to-all(f16[32,16,1152]{2,1,0:T(8,128)(2,1)S(1)} %bitcast.16), channel_id=1, replica_groups=mesh['x'=8,'yh'=4,'z'=8,'yl'=2,'core'=2] {'yh','x'}, dimensions={0} | all-to-all | bytes 2359296 | tf_op jit(solution)/shard_map/all_to_all | solution.py:14
  82.2 0.2 convert_reduce_fusion
  82.4 13.7 %all_to_all.42 = bf16[8,16,1152]{2,1,0:T(8,128)(2,1)S(1)} all-to-all(bf16[8,16,1152]{2,1,0:T(8,128)(2,1)S(1)} %broadcast_in_dim.17), channel_id=1, replica_groups=mesh['x'=8,'yh'=4,'z'=8,'yl'=2,'core'=2] {'x'}, dimensions={0} | all-to-all | bytes 589824 | tf_op jit(solution)/shard_map/all_to_all | solution.py:14
  96.2 0.1 broadcast_in_dim.18
  96.2 0.0 copy-start.3
  96.3 23.4 %all_to_all.43 = bf16[4,128,1152]{2,1,0:T(8,128)(2,1)S(1)} all-to-all(bf16[4,128,1152]{2,1,0:T(8,128)(2,1)S(1)} %broadcast_in_dim.18), channel_id=1, replica_groups=mesh['x'=8,'yh'=4,'z'=8,'yl'=2,'core'=2] {'yh'}, dimensions={0} | all-to-all | bytes 2359296 | tf_op jit(solution)/shard_map/all_to_all | solution.py:14
  119.7 0.0 copy-done.3
  119.7 1.2 fusion.3
  120.9 12.4 %all_to_all.44 = f32[2,16,16,576]{3,2,1,0:T(8,128)S(1)} all-to-all(f32[2,16,16,576]{3,2,1,0:T(8,128)S(1)} %bitcast.14), channel_id=1, replica_groups=mesh['x'=8,'yh'=4,'z'=8,'yl'=2,'core'=2] {'core'}, dimensions={0} | all-to-all | bytes 2359296 | tf_op jit(solution)/shard_map/all_to_all | solution.py:14
  133.3 0.0 copy-start.1
  133.3 0.0 copy-start.2
  133.3 0.8 fusion.2
  134.0 6.6 %all-to-all-start.5 = ((bf16[16,16,576]{2,1,0:T(8,128)(2,1)}), bf16[16,16,576]{2,1,0:T(8,128)(2,1)S(1)}, u32[]{:S(2)}, u32[]{:S(2)}) async-start(bf16[16,16,576]{2,1,0:T(8,128)(2,1)} %fusion.2), calls=%async_computation.5 | async-start | bytes 655360 | tf_op jit(solution)/shard_map/all_to_all | solution.py:14
  141.3 10.7 %all-to-all-done.5 = bf16[16,16,576]{2,1,0:T(8,128)(2,1)S(1)} async-done(((bf16[16,16,576]{2,1,0:T(8,128)(2,1)}), bf16[16,16,576]{2,1,0:T(8,128)(2,1)S(1)}, u32[]{:S(2)}, u32[]{:S(2)}) %all-to-all-start.5) | async-done | bytes 294944 | tf_op jit(solution)/shard_map/all_to_all | solution.py:14
  152.0 0.1 convert_reduce_fusion.1
  152.0 0.0 copy-done.1
  152.0 0.0 copy-done.2
  152.1 0.6 abs_reduce_fusion
  152.7 15.5 %all_to_all.45 = f32[32,1,576]{2,1,0:T(1,128)S(1)} all-to-all(f32[32,1,576]{2,1,0:T(1,128)S(1)} %broadcast_in_dim.19), channel_id=1, replica_groups=mesh['x'=8,'yh'=4,'z'=8,'yl'=2,'core'=2] {'x','yh'}, dimensions={0} | all-to-all | bytes 147456 | tf_op jit(solution)/shard_map/all_to_all | solution.py:14
  168.2 0.1 reduce_max.32
  168.3 15.1 %all_to_all.46 = f32[32,1,576]{2,1,0:T(1,128)S(1)} all-to-all(f32[32,1,576]{2,1,0:T(1,128)S(1)} %broadcast_in_dim.20), channel_id=1, replica_groups=mesh['x'=8,'yh'=4,'z'=8,'yl'=2,'core'=2] {'z','yl','core'}, dimensions={0} | all-to-all | bytes 147456 | tf_op jit(solution)/shard_map/all_to_all | solution.py:14
  183.4 0.8 reduce_max.33
  (4 shorter events, 0.1 us)
Async XLA Ops:
  0.6 34.7 %copy-start = (bf16[576,1152]{1,0:T(8,128)(2,1)S(1)}, bf16[576,1152]{1,0:T(8,128)(2,1)}, u32[]{:S(2)}) copy-start(bf16[576,1152]{1,0:T(8,128)(2,1)} %param.6) | copy-start | bytes 3981316
  96.2 23.4 %copy-start.3 = (bf16[1152,576]{0,1:T(8,128)(2,1)S(1)}, bf16[1152,576]{0,1:T(8,128)(2,1)}, u32[]{:S(2)}) copy-start(bf16[1152,576]{0,1:T(8,128)(2,1)} %param.7) | copy-start | bytes 3981316
  133.3 18.8 %copy-start.1 = (bf16[16,576]{1,0:T(8,128)(2,1)S(1)}, bf16[16,576]{1,0:T(8,128)(2,1)}, u32[]{:S(2)}) copy-start(bf16[16,576]{1,0:T(8,128)(2,1)} %param.5) | copy-start | bytes 55300
  133.3 18.8 %copy-start.2 = (s32[16,576]{1,0:T(8,128)S(1)}, s32[16,576]{1,0:T(8,128)}, u32[]{:S(2)}) copy-start(s32[16,576]{1,0:T(8,128)} %param.8) | copy-start | bytes 110596
  134.0 17.9 %all-to-all-start.5 = ((bf16[16,16,576]{2,1,0:T(8,128)(2,1)}), bf16[16,16,576]{2,1,0:T(8,128)(2,1)S(1)}, u32[]{:S(2)}, u32[]{:S(2)}) async-start(bf16[16,16,576]{2,1,0:T(8,128)(2,1)} %fusion.2), calls=%async_computation.5 | async-start | bytes 655360 | tf_op jit(solution)/shard_map/all_to_all | solution.py:14

commit v4 on v3

--- a/solution.py
+++ b/solution.py
@@ -7,6 +7,7 @@
 DP = ("x", "yh")
 TENSOR = ("z", "yl", "core")
 LIFT = 128.0
+LOW_LIFT = 16.0
 ROW_MAJOR = Layout(major_to_minor=(0, 1))
 
 
@@ -29,11 +30,13 @@
     half = gather(tokens, ("z", "yl"), 16)
     gathered = lax.all_gather(half, "core", axis=0, tiled=True)
     hidden_part = jnp.dot(gathered, up_weight, preferred_element_type=jnp.float32)
-    hidden_part = (hidden_part * LIFT).astype(jnp.float16).reshape(32, rows, shards)
-    hidden = jnp.sum(exchange(hidden_part, ("yh", "x")).astype(jnp.float32), axis=0) * (1.0 / LIFT)
+    hidden_part = (hidden_part * LIFT).astype(jnp.float16).reshape(8, 4 * rows, shards)
+    hidden_part = jnp.sum(exchange(hidden_part, "x").astype(jnp.float32), axis=0)
+    hidden_part = (hidden_part * (LOW_LIFT / LIFT)).astype(jnp.float16)
+    spread = exchange(jnp.broadcast_to(hidden_part, (4,) + hidden_part.shape), "yh")
+    hidden = jnp.sum(spread.astype(jnp.float32), axis=0) * (1.0 / LOW_LIFT)
     positive = jnp.maximum(hidden, 0.0)
     active = gather((positive * positive).astype(jnp.bfloat16), "x", 8)
-    active = gather(active, "yh", 4)
     out_part = jnp.dot(active, down_weight, preferred_element_type=jnp.float32)
     out_part = with_layout_constraint(out_part, ROW_MAJOR)
     pair = exchange(out_part.reshape(2, 16, rows, width), "core")

time: 185 us -> 185 us (level)
  starting transfers between devices: 6.63 us -> 4.57 us
  blocking collectives: 160 us -> 162 us
    all_to_all x7, blocking collectives: 155 us -> 158 us  [exchange(): return lax.all_to_all(blocks, axes, split_axis=0, concat_axis=0, tiled=True)]
    all_to_all x1, starting transfers between devices: 6.63 us -> 4.57 us  [exchange(): return lax.all_to_all(blocks, axes, split_axis=0, concat_axis=0, tiled=True)]
where the time goes in v4:
time: 185 us
  blocking collectives  162 us (88%)
  waiting for transfers between devices  10.7 us (6%)
  starting transfers between devices  4.57 us (2%)
  other arithmetic  2.61 us (1%)
  matrix products  2.33 us (1%)
    all_to_all x7, blocking collectives, exchange(): return lax.all_to_all(blocks, axes, split_axis=0, concat_axis=0, tiled=True)  158 us
    all_to_all x1, waiting for transfers between devices, exchange(): return lax.all_to_all(blocks, axes, split_axis=0, concat_axis=0, tiled=True)  10.7 us
    all_to_all x1, starting transfers between devices, exchange(): return lax.all_to_all(blocks, axes, split_axis=0, concat_axis=0, tiled=True)  4.57 us
    all_gather x1, blocking collectives, body(): gathered = lax.all_gather(half, 'core', axis=0, tiled=True)  4.35 us
  transfers between devices with their start and end apart: 1, of which 1 were waited for; matrix products, arithmetic and copies ran while one was open for 0% of the time, Pallas kernels for 0%

profile of v4, /device:TPU:1, one launch (start us, length us, event | category | flops | bytes accessed | tf_op | source)
XLA Modules:
  0.0 184.8 jit_solution(463713883036175936)
XLA Ops:
  0.6 0.0 copy-start
  0.6 0.9 broadcast_in_dim.16
  1.5 29.5 %all_to_all.40 = bf16[16,16,576]{2,1,0:T(8,128)(2,1)S(1)} all-to-all(bf16[16,16,576]{2,1,0:T(8,128)(2,1)S(1)} %broadcast_in_dim.16), channel_id=1, replica_groups=mesh['x'=8,'yh'=4,'z'=8,'yl'=2,'core'=2] {'z','yl'}, dimensions={0} | all-to-all | bytes 589824 | tf_op jit(solution)/shard_map/all_to_all | solution.py:15
  31.0 4.3 %all_gather.3 = bf16[512,576]{1,0:T(8,128)(2,1)S(1)} all-gather(bf16[256,576]{1,0:T(8,128)(2,1)S(1)} %bitcast.14), channel_id=1, replica_groups=mesh['x'=8,'yh'=4,'z'=8,'yl'=2,'core'=2] {'core'}, dimensions={0}, use_global_device_ids=true | all-gather | bytes 884736 | tf_op jit(solution)/shard_map/all_gather | solution.py:31
  35.3 0.0 copy-done
  35.3 1.2 fusion
  36.5 37.0 %all_to_all.41 = f16[8,64,1152]{2,1,0:T(8,128)(2,1)S(1)} all-to-all(f16[8,64,1152]{2,1,0:T(8,128)(2,1)S(1)} %bitcast.15), channel_id=1, replica_groups=mesh['x'=8,'yh'=4,'z'=8,'yl'=2,'core'=2] {'x'}, dimensions={0} | all-to-all | bytes 2359296 | tf_op jit(solution)/shard_map/all_to_all | solution.py:15
  73.5 0.2 convert_reduce_fusion
  73.7 21.7 %all_to_all.42 = f16[4,64,1152]{2,1,0:T(8,128)(2,1)S(1)} all-to-all(f16[4,64,1152]{2,1,0:T(8,128)(2,1)S(1)} %broadcast_in_dim.17), channel_id=1, replica_groups=mesh['x'=8,'yh'=4,'z'=8,'yl'=2,'core'=2] {'yh'}, dimensions={0} | all-to-all | bytes 1179648 | tf_op jit(solution)/shard_map/all_to_all | solution.py:15
  95.5 0.1 convert_reduce_fusion.1
  95.6 0.1 broadcast_in_dim.18
  95.8 0.0 copy-start.3
  95.8 30.5 %all_to_all.43 = bf16[8,64,1152]{2,1,0:T(8,128)(2,1)S(1)} all-to-all(bf16[8,64,1152]{2,1,0:T(8,128)(2,1)S(1)} %broadcast_in_dim.18), channel_id=1, replica_groups=mesh['x'=8,'yh'=4,'z'=8,'yl'=2,'core'=2] {'x'}, dimensions={0} | all-to-all | bytes 2359296 | tf_op jit(solution)/shard_map/all_to_all | solution.py:15
  126.3 0.0 copy-done.3
  126.3 1.2 fusion.3
  127.5 9.2 %all_to_all.44 = f32[2,16,16,576]{3,2,1,0:T(8,128)S(1)} all-to-all(f32[2,16,16,576]{3,2,1,0:T(8,128)S(1)} %bitcast.13), channel_id=1, replica_groups=mesh['x'=8,'yh'=4,'z'=8,'yl'=2,'core'=2] {'core'}, dimensions={0} | all-to-all | bytes 2359296 | tf_op jit(solution)/shard_map/all_to_all | solution.py:15
  136.7 0.0 copy-start.1
  136.7 0.0 copy-start.2
  136.7 0.8 fusion.2
  137.5 4.6 %all-to-all-start.5 = ((bf16[16,16,576]{2,1,0:T(8,128)(2,1)}), bf16[16,16,576]{2,1,0:T(8,128)(2,1)S(1)}, u32[]{:S(2)}, u32[]{:S(2)}) async-start(bf16[16,16,576]{2,1,0:T(8,128)(2,1)} %fusion.2), calls=%async_computation.5 | async-start | bytes 655360 | tf_op jit(solution)/shard_map/all_to_all | solution.py:15
  142.7 10.7 %all-to-all-done.5 = bf16[16,16,576]{2,1,0:T(8,128)(2,1)S(1)} async-done(((bf16[16,16,576]{2,1,0:T(8,128)(2,1)}), bf16[16,16,576]{2,1,0:T(8,128)(2,1)S(1)}, u32[]{:S(2)}, u32[]{:S(2)}) %all-to-all-start.5) | async-done | bytes 294944 | tf_op jit(solution)/shard_map/all_to_all | solution.py:15
  153.3 0.1 convert_reduce_fusion.2
  153.4 0.0 copy-done.1
  153.4 0.0 copy-done.2
  153.4 0.6 abs_reduce_fusion
  154.1 15.0 %all_to_all.45 = f32[32,1,576]{2,1,0:T(1,128)S(1)} all-to-all(f32[32,1,576]{2,1,0:T(1,128)S(1)} %broadcast_in_dim.19), channel_id=1, replica_groups=mesh['x'=8,'yh'=4,'z'=8,'yl'=2,'core'=2] {'x','yh'}, dimensions={0} | all-to-all | bytes 147456 | tf_op jit(solution)/shard_map/all_to_all | solution.py:15
  169.0 0.1 reduce_max.32
  169.2 14.8 %all_to_all.46 = f32[32,1,576]{2,1,0:T(1,128)S(1)} all-to-all(f32[32,1,576]{2,1,0:T(1,128)S(1)} %broadcast_in_dim.20), channel_id=1, replica_groups=mesh['x'=8,'yh'=4,'z'=8,'yl'=2,'core'=2] {'z','yl','core'}, dimensions={0} | all-to-all | bytes 147456 | tf_op jit(solution)/shard_map/all_to_all | solution.py:15
  184.0 0.8 reduce_max.33
  (5 shorter events, 0.2 us)
Async XLA Ops:
  0.6 34.7 %copy-start = (bf16[576,1152]{1,0:T(8,128)(2,1)S(1)}, bf16[576,1152]{1,0:T(8,128)(2,1)}, u32[]{:S(2)}) copy-start(bf16[576,1152]{1,0:T(8,128)(2,1)} %param.6) | copy-start | bytes 3981316
  95.8 30.6 %copy-start.3 = (bf16[1152,576]{0,1:T(8,128)(2,1)S(1)}, bf16[1152,576]{0,1:T(8,128)(2,1)}, u32[]{:S(2)}) copy-start(bf16[1152,576]{0,1:T(8,128)(2,1)} %param.7) | copy-start | bytes 3981316
  136.7 16.7 %copy-start.1 = (bf16[16,576]{1,0:T(8,128)(2,1)S(1)}, bf16[16,576]{1,0:T(8,128)(2,1)}, u32[]{:S(2)}) copy-start(bf16[16,576]{1,0:T(8,128)(2,1)} %param.5) | copy-start | bytes 55300
  136.7 16.7 %copy-start.2 = (s32[16,576]{1,0:T(8,128)S(1)}, s32[16,576]{1,0:T(8,128)}, u32[]{:S(2)}) copy-start(s32[16,576]{1,0:T(8,128)} %param.8) | copy-start | bytes 110596
  137.5 15.9 %all-to-all-start.5 = ((bf16[16,16,576]{2,1,0:T(8,128)(2,1)}), bf16[16,16,576]{2,1,0:T(8,128)(2,1)S(1)}, u32[]{:S(2)}, u32[]{:S(2)}) async-start(bf16[16,16,576]{2,1,0:T(8,128)(2,1)} %fusion.2), calls=%async_computation.5 | async-start | bytes 655360 | tf_op jit(solution)/shard_map/all_to_all | solution.py:15

commit v5 on v3

--- a/solution.py
+++ b/solution.py
@@ -23,24 +23,35 @@
     return jnp.max(exchange(jnp.broadcast_to(values, (n,) + values.shape), axes), axis=0)
 
 
+def lane_maxima(values):
+    lanes = 128
+    tail = values.shape[1] % lanes
+    largest = jnp.max(jnp.pad(values[:, values.shape[1] - tail :], ((0, 0), (0, lanes - tail))), axis=0)
+    for low in range(0, values.shape[1] - tail, lanes):
+        largest = jnp.maximum(largest, jnp.max(values[:, low : low + lanes], axis=0))
+    return largest[None]
+
+
 def body(tokens, up_weight, down_weight, keep_bits, prior_scale):
     rows, width = tokens.shape
     shards = up_weight.shape[1]
+    first, tokens = lax.optimization_barrier((lax.axis_index("core") == 0, tokens))
     half = gather(tokens, ("z", "yl"), 16)
     gathered = lax.all_gather(half, "core", axis=0, tiled=True)
     hidden_part = jnp.dot(gathered, up_weight, preferred_element_type=jnp.float32)
     hidden_part = (hidden_part * LIFT).astype(jnp.float16).reshape(32, rows, shards)
-    hidden = jnp.sum(exchange(hidden_part, ("yh", "x")).astype(jnp.float32), axis=0) * (1.0 / LIFT)
+    hidden = jnp.sum(exchange(hidden_part, DP).astype(jnp.float32), axis=0) * (1.0 / LIFT)
     positive = jnp.maximum(hidden, 0.0)
-    active = gather((positive * positive).astype(jnp.bfloat16), "x", 8)
-    active = gather(active, "yh", 4)
+    active = gather((positive * positive).astype(jnp.bfloat16), DP, 32)
     out_part = jnp.dot(active, down_weight, preferred_element_type=jnp.float32)
     out_part = with_layout_constraint(out_part, ROW_MAJOR)
-    pair = exchange(out_part.reshape(2, 16, rows, width), "core")
-    out_part = (pair[0] + pair[1]).astype(jnp.bfloat16)
+    low, high = out_part[: 16 * rows], out_part[16 * rows :]
+    swapped = lax.all_gather(jnp.where(first, high, low).astype(jnp.bfloat16), "core", axis=0)
+    other = jnp.where(first, swapped[1], swapped[0]).astype(jnp.float32)
+    out_part = (jnp.where(first, low, high) + other).astype(jnp.bfloat16).reshape(16, rows, width)
     mlp_out = jnp.sum(exchange(out_part, ("z", "yl")).astype(jnp.float32), axis=0)
     combined = tokens.astype(jnp.float32) + keep_bits.astype(jnp.float32) * mlp_out / 0.9
-    largest = jnp.max(jnp.abs(combined), axis=0, keepdims=True)
+    largest = lane_maxima(jnp.abs(combined))
     amax = jnp.max(max_over(max_over(largest, DP, 32), TENSOR, 32)).reshape(1)
     scaled = jnp.clip(combined * prior_scale[0], -448.0, 448.0).astype(jnp.bfloat16)
     return (scaled, amax)

time: 185 us -> 173 us (0.935)
  blocking collectives: 160 us -> 151 us
  starting transfers between devices: 6.63 us -> 3.54 us
    all_to_all x7 -> x5, blocking collectives: 155 us -> 141 us  [exchange(): return lax.all_to_all(blocks, axes, split_axis=0, concat_axis=0, tiled=True)]
    all_gather x0 -> x1, blocking collectives: none -> 5.74 us  [body(): lax.all_gather(jnp.where(first, high, low).astype(jnp.bfloat16), 'core',...]
    all_to_all x1, starting transfers between devices: 6.63 us -> 3.54 us  [exchange(): return lax.all_to_all(blocks, axes, split_axis=0, concat_axis=0, tiled=True)]
where the time goes in v5:
time: 173 us; the launch traced here: 172 us
  blocking collectives  151 us (87%)
  waiting for transfers between devices  10.7 us (6%)
  starting transfers between devices  3.54 us (2%)
  other arithmetic  2.47 us (1%)
  matrix products  2.34 us (1%)
    all_to_all x5, blocking collectives, exchange(): return lax.all_to_all(blocks, axes, split_axis=0, concat_axis=0, tiled=True)  141 us
    all_to_all x1, waiting for transfers between devices, exchange(): return lax.all_to_all(blocks, axes, split_axis=0, concat_axis=0, tiled=True)  10.7 us
    all_gather x1, blocking collectives, body(): lax.all_gather(jnp.where(first, high, low).astype(jnp.bfloat16), 'core',...  5.74 us
    all_gather x1, blocking collectives, body(): gathered = lax.all_gather(half, 'core', axis=0, tiled=True)  4.35 us
    all_to_all x1, starting transfers between devices, exchange(): return lax.all_to_all(blocks, axes, split_axis=0, concat_axis=0, tiled=True)  3.54 us
  transfers between devices with their start and end apart: 1, of which 1 were waited for; matrix products, arithmetic and copies ran while one was open for 0% of the time, Pallas kernels for 0%

profile of v5, /device:TPU:1, one launch (start us, length us, event | category | flops | bytes accessed | tf_op | source)
XLA Modules:
  0.0 172.1 jit_solution(11587583962631637516)
XLA Ops:
  0.6 0.0 copy-start
  0.7 0.9 broadcast_in_dim.13
  1.5 29.5 %all_to_all.30 = bf16[16,16,576]{2,1,0:T(8,128)(2,1)S(1)} all-to-all(bf16[16,16,576]{2,1,0:T(8,128)(2,1)S(1)} %broadcast_in_dim.13), channel_id=1, replica_groups=mesh['x'=8,'yh'=4,'z'=8,'yl'=2,'core'=2] {'z','yl'}, dimensions={0} | all-to-all | bytes 589824 | tf_op jit(solution)/shard_map/all_to_all | solution.py:14
  31.0 4.3 %all_gather.9 = bf16[512,576]{1,0:T(8,128)(2,1)S(1)} all-gather(bf16[256,576]{1,0:T(8,128)(2,1)S(1)} %bitcast.13), channel_id=1, replica_groups=mesh['x'=8,'yh'=4,'z'=8,'yl'=2,'core'=2] {'core'}, dimensions={0}, use_global_device_ids=true | all-gather | bytes 884736 | tf_op jit(solution)/shard_map/all_gather | solution.py:40
  35.3 0.0 copy-done
  35.3 1.2 fusion
  36.5 44.7 %all_to_all.31 = f16[32,16,1152]{2,1,0:T(8,128)(2,1)S(1)} all-to-all(f16[32,16,1152]{2,1,0:T(8,128)(2,1)S(1)} %bitcast.14), channel_id=1, replica_groups=mesh['x'=8,'yh'=4,'z'=8,'yl'=2,'core'=2] {'x','yh'}, dimensions={0} | all-to-all | bytes 2359296 | tf_op jit(solution)/shard_map/all_to_all | solution.py:14
  81.2 0.2 convert_reduce_fusion
  81.4 0.1 broadcast_in_dim.14
  81.5 0.0 copy-start.3
  81.5 36.5 %all_to_all.32 = bf16[32,16,1152]{2,1,0:T(8,128)(2,1)S(1)} all-to-all(bf16[32,16,1152]{2,1,0:T(8,128)(2,1)S(1)} %broadcast_in_dim.14), channel_id=1, replica_groups=mesh['x'=8,'yh'=4,'z'=8,'yl'=2,'core'=2] {'x','yh'}, dimensions={0} | all-to-all | bytes 2359296 | tf_op jit(solution)/shard_map/all_to_all | solution.py:14
  118.0 0.0 copy-done.3
  118.0 1.2 fusion.3
  119.2 0.1 select_convert_fusion
  119.3 5.7 %all-gather = bf16[512,576]{1,0:T(8,128)(2,1)S(1)} all-gather(bf16[256,576]{1,0:T(8,128)(2,1)S(1)} %select_convert_fusion), channel_id=2, replica_groups=mesh['x'=8,'yh'=4,'z'=8,'yl'=2,'core'=2] {'core'}, dimensions={0}, use_global_device_ids=true | all-gather | bytes 884736 | tf_op jit(solution)/shard_map/all_gather | solution.py:49
  125.0 0.0 copy-start.1
  125.0 0.0 copy-start.2
  125.1 0.9 fusion.1
  125.9 3.5 %all-to-all-start.3 = ((bf16[16,16,576]{2,1,0:T(8,128)(2,1)}), bf16[16,16,576]{2,1,0:T(8,128)(2,1)S(1)}, u32[]{:S(2)}, u32[]{:S(2)}) async-start(bf16[16,16,576]{2,1,0:T(8,128)(2,1)} %bitcast.3), calls=%async_computation.3 | async-start | bytes 655360 | tf_op jit(solution)/shard_map/all_to_all | solution.py:14
  130.1 10.7 %all-to-all-done.3 = bf16[16,16,576]{2,1,0:T(8,128)(2,1)S(1)} async-done(((bf16[16,16,576]{2,1,0:T(8,128)(2,1)}), bf16[16,16,576]{2,1,0:T(8,128)(2,1)S(1)}, u32[]{:S(2)}, u32[]{:S(2)}) %all-to-all-start.3) | async-done | bytes 294944 | tf_op jit(solution)/shard_map/all_to_all | solution.py:14
  140.8 0.1 convert_reduce_fusion.1
  140.8 0.0 copy-done.1
  140.9 0.0 copy-done.2
  140.9 0.6 fusion.2
  141.5 15.4 %all_to_all.33 = f32[32,1,128]{2,1,0:T(1,128)S(1)} all-to-all(f32[32,1,128]{2,1,0:T(1,128)S(1)} %broadcast_in_dim.15), channel_id=1, replica_groups=mesh['x'=8,'yh'=4,'z'=8,'yl'=2,'core'=2] {'x','yh'}, dimensions={0} | all-to-all | bytes 32768 | tf_op jit(solution)/shard_map/all_to_all | solution.py:14
  157.0 14.5 %all_to_all.34 = f32[32,1,128]{2,1,0:T(1,128)S(1)} all-to-all(f32[32,1,128]{2,1,0:T(1,128)S(1)} %broadcast_in_dim.16), channel_id=1, replica_groups=mesh['x'=8,'yh'=4,'z'=8,'yl'=2,'core'=2] {'z','yl','core'}, dimensions={0} | all-to-all | bytes 32768 | tf_op jit(solution)/shard_map/all_to_all | solution.py:14
  171.5 0.6 reduce_max.73
  (7 shorter events, 0.1 us)
Async XLA Ops:
  0.6 34.7 %copy-start = (bf16[576,1152]{1,0:T(8,128)(2,1)S(1)}, bf16[576,1152]{1,0:T(8,128)(2,1)}, u32[]{:S(2)}) copy-start(bf16[576,1152]{1,0:T(8,128)(2,1)} %param.6) | copy-start | bytes 3981316
  81.5 36.5 %copy-start.3 = (bf16[1152,576]{0,1:T(8,128)(2,1)S(1)}, bf16[1152,576]{0,1:T(8,128)(2,1)}, u32[]{:S(2)}) copy-start(bf16[1152,576]{0,1:T(8,128)(2,1)} %param.7) | copy-start | bytes 3981316
  125.0 15.8 %copy-start.1 = (bf16[16,576]{1,0:T(8,128)(2,1)S(1)}, bf16[16,576]{1,0:T(8,128)(2,1)}, u32[]{:S(2)}) copy-start(bf16[16,576]{1,0:T(8,128)(2,1)} %param.5) | copy-start | bytes 55300
  125.0 15.8 %copy-start.2 = (s32[16,576]{1,0:T(8,128)S(1)}, s32[16,576]{1,0:T(8,128)}, u32[]{:S(2)}) copy-start(s32[16,576]{1,0:T(8,128)} %param.8) | copy-start | bytes 110596
  125.9 14.8 %all-to-all-start.3 = ((bf16[16,16,576]{2,1,0:T(8,128)(2,1)}), bf16[16,16,576]{2,1,0:T(8,128)(2,1)S(1)}, u32[]{:S(2)}, u32[]{:S(2)}) async-start(bf16[16,16,576]{2,1,0:T(8,128)(2,1)} %bitcast.3), calls=%async_computation.3 | async-start | bytes 655360 | tf_op jit(solution)/shard_map/all_to_all | solution.py:14

commit v6 on v5

v6 whole, which is shorter than its diff:
```python
import jax
import jax.numpy as jnp
from jax import lax
from jax.experimental.layout import Layout, with_layout_constraint
from jax.sharding import Mesh, PartitionSpec as P

DP = ("xp", "xh", "yh")
TENSOR = ("z", "yl", "core")
LIKE = ("xp", "yh")
LIFT = 64.0
ROW_MAJOR = Layout(major_to_minor=(0, 1))


def exchange(blocks, axes):
    return lax.all_to_all(blocks, axes, split_axis=0, concat_axis=0, tiled=True)


def gather(block, axes, n):
    spread = exchange(jnp.broadcast_to(block, (n,) + block.shape), axes)
    return spread.reshape((n * block.shape[0],) + block.shape[1:])


def max_over(values, axes, n):
    return jnp.max(exchange(jnp.broadcast_to(values, (n,) + values.shape), axes), axis=0)


def lane_maxima(values):
    lanes = 128
    tail = values.shape[1] % lanes
    largest = jnp.max(jnp.pad(values[:, values.shape[1] - tail :], ((0, 0), (0, lanes - tail))), axis=0)
    for low in range(0, values.shape[1] - tail, lanes):
        largest = jnp.maximum(largest, jnp.max(values[:, low : low + lanes], axis=0))
    return largest[None]


def partner(x, n):
    return (x + 1) % n if x % 2 else (x - 1) % n


def body(tokens, up_weight, down_weight, keep_bits, prior_scale):
    rows, width = tokens.shape
    shards = up_weight.shape[1]
    n = 2 * lax.axis_size("xp")
    blocks = lax.axis_size("z") * lax.axis_size("yl")
    core = lax.axis_index("core")
    first, same, tokens = lax.optimization_barrier((core == 0, core == lax.axis_index("xh"), tokens))
    moves = []
    for x in range(n):
        moves.append((2 * x + x % 2, 2 * x))
        moves.append((2 * x + 1 - x % 2, 2 * partner(x, n) + 1))
    chosen = lax.ppermute(tokens, ("xp", "xh", "core"), moves)
    chosen, up_sent, down_sent = lax.optimization_barrier((chosen, up_weight, down_weight))
    up_other = lax.ppermute(up_sent, ("xp", "xh"), [(x, partner(x, n)) for x in range(n)])
    down_other = lax.ppermute(down_sent, "xh", [(0, 1), (1, 0)])
    half = gather(chosen, ("z", "yl"), blocks)
    both = lax.all_gather(half, "core", axis=0, tiled=True)
    near, far = both[: blocks * rows], both[blocks * rows :]
    hidden_part = jnp.dot(near, up_weight, preferred_element_type=jnp.float32)
    hidden_part = hidden_part + jnp.dot(far, up_other, preferred_element_type=jnp.float32)
    hidden_part = (hidden_part * LIFT).astype(jnp.float16).reshape(blocks, rows, shards)
    hidden_part, down_other = lax.optimization_barrier((hidden_part, down_other))
    hidden = jnp.sum(exchange(hidden_part, LIKE).astype(jnp.float32), axis=0) * (1.0 / LIFT)
    positive = jnp.maximum(hidden, 0.0)
    active = gather((positive * positive).astype(jnp.bfloat16), LIKE, blocks)
    mine = with_layout_constraint(jnp.dot(active, down_weight, preferred_element_type=jnp.float32), ROW_MAJOR)
    theirs = with_layout_constraint(jnp.dot(active, down_other, preferred_element_type=jnp.float32), ROW_MAJOR)
    swapped = lax.all_gather(jnp.where(same, theirs, mine).astype(jnp.bfloat16), "core", axis=0)
    other = jnp.where(first, swapped[1], swapped[0]).astype(jnp.float32)
    out_part = (jnp.where(same, mine, theirs) + other).astype(jnp.bfloat16).reshape(blocks, rows, width)
    mlp_out = jnp.sum(exchange(out_part, ("z", "yl")).astype(jnp.float32), axis=0)
    mlp_out = lax.ppermute(mlp_out, ("xh", "core"), [(0, 0), (1, 2), (2, 1), (3, 3)])
    combined = tokens.astype(jnp.float32) + keep_bits.astype(jnp.float32) * mlp_out / 0.9
    largest = lane_maxima(jnp.abs(combined))
    amax = jnp.max(max_over(max_over(largest, DP, n * lax.axis_size("yh")), TENSOR, 2 * blocks)).reshape(1)
    scaled = jnp.clip(combined * prior_scale[0], -448.0, 448.0).astype(jnp.bfloat16)
    return (scaled, amax)


def solution(mesh):
    fine = Mesh(mesh.devices.reshape(4, 2, 4, 8, 2, 2), DP + TENSOR)
    return jax.shard_map(
        body,
        mesh=fine,
        in_specs=(P(TENSOR, DP), P(DP, TENSOR), P(TENSOR, DP), P(TENSOR, DP), P()),
        out_specs=(P(TENSOR, DP), P()),
        check_vma=False,
    )
```

time: 173 us -> 173 us (level)
  starting transfers between devices: 3.54 us -> 13 us
  waiting for transfers between devices: 10.7 us -> 4.97 us
  blocking collectives: 151 us -> 149 us
    ppermute x0 -> x4, starting transfers between devices: none -> 13 us  [the longest x1 5.46 us: body(): chosen = lax.ppermute(tokens, ('xp', 'xh', 'core'), moves)]
    all_to_all x1 -> x0, waiting for transfers between devices: 10.7 us -> none  [exchange(): return lax.all_to_all(blocks, axes, split_axis=0, concat_axis=0, tiled=True)]
    ppermute x0 -> x4, waiting for transfers between devices: none -> 4.97 us  [the longest x1 2.75 us: body(): lax.ppermute(mlp_out, ('xh', 'core'), [(0, 0), (1, 2), (2, 1), (3, 3)])]
    all_to_all x1 -> x0, starting transfers between devices: 3.54 us -> none  [exchange(): return lax.all_to_all(blocks, axes, split_axis=0, concat_axis=0, tiled=True)]
    all_to_all x5 -> x6, blocking collectives: 141 us -> 140 us  [exchange(): return lax.all_to_all(blocks, axes, split_axis=0, concat_axis=0, tiled=True)]
  transfers between devices with their start and end apart: 1 -> 4, of which waited for: 1 -> 2; matrix products, arithmetic and copies ran while one was open for 0% -> 1% of each run, Pallas kernels for 0% -> 0%
where the time goes in v6:
time: 173 us
  blocking collectives  149 us (86%)
  starting transfers between devices  13 us (8%)
  waiting for transfers between devices  4.97 us (3%)
  matrix products  2.69 us (2%)
    all_to_all x6, blocking collectives, exchange(): return lax.all_to_all(blocks, axes, split_axis=0, concat_axis=0, tiled=True)  140 us
    all_gather x1, blocking collectives, body(): lax.all_gather(jnp.where(same, theirs, mine).astype(jnp.bfloat16), 'core'...  6.59 us
    ppermute x1, starting transfers between devices, body(): chosen = lax.ppermute(tokens, ('xp', 'xh', 'core'), moves)  5.46 us
    ppermute x1, starting transfers between devices, body(): lax.ppermute(up_sent, ('xp', 'xh'), [(x, partner(x, n)) for x in range(n)])  3.74 us
  transfers between devices with their start and end apart: 4, of which 2 were waited for; matrix products, arithmetic and copies ran while one was open for 1% of the time, Pallas kernels for 0%

profile of v6, /device:TPU:1, one launch (start us, length us, event | category | flops | bytes accessed | tf_op | source)
XLA Modules:
  0.0 172.8 jit_solution(9038683154511728975)
XLA Ops:
  0.6 0.0 copy-start.1
  0.6 5.5 %collective-permute-start = (bf16[16,576]{1,0:T(8,128)(2,1)}, bf16[16,576]{1,0:T(8,128)(2,1)S(1)}, u32[]{:S(2)}, u32[]{:S(2)}) collective-permute-start(bf16[16,576]{1,0:T(8,128)(2,1)} %param.5), channel_id=1, source_target_pairs={{0,0},{1,897},{129,128},{128,257},{256,256},{257,129},{385,384},{3... | collective-permute-start | bytes 55304 | tf_op jit(solution)/shard_map/ppermute | solution.py:51
  6.1 2.2 %collective-permute-done = bf16[16,576]{1,0:T(8,128)(2,1)S(1)} collective-permute-done((bf16[16,576]{1,0:T(8,128)(2,1)}, bf16[16,576]{1,0:T(8,128)(2,1)S(1)}, u32[]{:S(2)}, u32[]{:S(2)}) %collective-permute-start) | collective-permute-done | bytes 18464 | tf_op jit(solution)/shard_map/ppermute | solution.py:51
  8.3 3.7 %collective-permute-start.1 = (bf16[576,1152]{1,0:T(8,128)(2,1)}, bf16[576,1152]{1,0:T(8,128)(2,1)S(1)}, u32[]{:S(2)}, u32[]{:S(2)}) collective-permute-start(bf16[576,1152]{1,0:T(8,128)(2,1)} %param.6), channel_id=1, source_target_pairs={{0,896},{128,256},{256,128},{384,512},{512,384},{640,768},{768,640... | collective-permute-start | bytes 3981320 | tf_op jit(solution)/shard_map/ppermute | solution.py:53
  12.1 1.9 %collective-permute-start.2 = (bf16[1152,576]{0,1:T(8,128)(2,1)}, bf16[1152,576]{0,1:T(8,128)(2,1)S(1)}, u32[]{:S(2)}, u32[]{:S(2)}) collective-permute-start(bf16[1152,576]{0,1:T(8,128)(2,1)} %param.7), channel_id=1, source_target_pairs={{0,128},{128,0},{1,129},{129,1},{2,130},{130,2},{3,131},{131,3},{4... | collective-permute-start | bytes 3981320 | tf_op jit(solution)/shard_map/ppermute | solution.py:54
  14.1 30.0 %all_to_all.30 = bf16[16,16,576]{2,1,0:T(8,128)(2,1)S(1)} all-to-all(bf16[16,16,576]{2,1,0:T(8,128)(2,1)S(1)} %broadcast_in_dim.13), channel_id=1, replica_groups=mesh['xp'=4,'xh'=2,'yh'=4,'z'=8,'yl'=2,'core'=2] {'z','yl'}, dimensions={0} | all-to-all | bytes 589824 | tf_op jit(solution)/shard_map/all_to_all | solution.py:15
  44.0 2.3 %all_gather.9 = bf16[512,576]{1,0:T(8,128)(2,1)S(1)} all-gather(bf16[256,576]{1,0:T(8,128)(2,1)S(1)} %bitcast.18), channel_id=1, replica_groups=mesh['xp'=4,'xh'=2,'yh'=4,'z'=8,'yl'=2,'core'=2] {'core'}, dimensions={0}, use_global_device_ids=true | all-gather | bytes 884736 | tf_op jit(solution)/shard_map/all_gather | solution.py:56
  46.3 0.0 copy-done.1
  46.3 0.6 fusion.4
  46.9 0.0 collective-permute-done.1
  47.0 0.6 fusion.1
  47.6 0.0 collective-permute-done.2
  47.6 28.0 %all_to_all.31 = f16[16,16,1152]{2,1,0:T(8,128)(2,1)S(1)} all-to-all(f16[16,16,1152]{2,1,0:T(8,128)(2,1)S(1)} %bitcast.17), channel_id=1, replica_groups=mesh['xp'=4,'xh'=2,'yh'=4,'z'=8,'yl'=2,'core'=2] {'xp','yh'}, dimensions={0} | all-to-all | bytes 1179648 | tf_op jit(solution)/shard_map/all_to_all | solution.py:15
  75.6 0.0 copy-start
  75.6 0.1 convert_reduce_fusion
  75.8 26.9 %all_to_all.32 = bf16[16,16,1152]{2,1,0:T(8,128)(2,1)S(1)} all-to-all(bf16[16,16,1152]{2,1,0:T(8,128)(2,1)S(1)} %broadcast_in_dim.14), channel_id=1, replica_groups=mesh['xp'=4,'xh'=2,'yh'=4,'z'=8,'yl'=2,'core'=2] {'xp','yh'}, dimensions={0} | all-to-all | bytes 1179648 | tf_op jit(solution)/shard_map/all_to_all | solution.py:15
  102.7 0.0 copy-done
  102.7 0.7 fusion.7
  103.4 0.7 select_convert_fusion
  104.1 6.6 %all-gather = bf16[512,576]{1,0:T(8,128)(2,1)S(1)} all-gather(bf16[256,576]{1,0:T(8,128)(2,1)S(1)} %get-tuple-element.24), channel_id=2, replica_groups=mesh['xp'=4,'xh'=2,'yh'=4,'z'=8,'yl'=2,'core'=2] {'core'}, dimensions={0}, use_global_device_ids=true | all-gather | bytes 884736 | tf_op jit(solution)/shard_map/all_gather | solution.py:67
  110.7 0.0 copy-start.2
  110.7 0.0 copy-start.3
  110.7 0.2 fusion.2
  110.8 26.1 %all_to_all.33 = bf16[16,16,576]{2,1,0:T(8,128)(2,1)S(1)} all-to-all(bf16[16,16,576]{2,1,0:T(8,128)(2,1)S(1)} %bitcast.19), channel_id=1, replica_groups=mesh['xp'=4,'xh'=2,'yh'=4,'z'=8,'yl'=2,'core'=2] {'z','yl'}, dimensions={0} | all-to-all | bytes 589824 | tf_op jit(solution)/shard_map/all_to_all | solution.py:15
  136.9 0.1 convert_reduce_fusion.1
  137.0 1.9 %collective-permute-start.3 = (f32[16,576]{1,0:T(8,128)S(1)}, f32[16,576]{1,0:T(8,128)S(1)}, u32[]{:S(2)}, u32[]{:S(2)}) collective-permute-start(f32[16,576]{1,0:T(8,128)S(1)} %convert_reduce_fusion.1), channel_id=1, source_target_pairs={{0,0},{1,128},{128,1},{129,129},{2,2},{3,130},{130,3},{131,131},{4... | collective-permute-start | bytes 110600 | tf_op jit(solution)/shard_map/ppermute | solution.py:71
  139.6 2.7 %collective-permute-done.3 = f32[16,576]{1,0:T(8,128)S(1)} collective-permute-done((f32[16,576]{1,0:T(8,128)S(1)}, f32[16,576]{1,0:T(8,128)S(1)}, u32[]{:S(2)}, u32[]{:S(2)}) %collective-permute-start.3) | collective-permute-done | bytes 36896 | tf_op jit(solution)/shard_map/ppermute | solution.py:71
  142.3 0.0 copy-done.2
  142.3 0.0 copy-done.3
  142.3 0.6 fusion.6
  143.0 15.9 %all_to_all.34 = f32[32,1,128]{2,1,0:T(1,128)S(1)} all-to-all(f32[32,1,128]{2,1,0:T(1,128)S(1)} %broadcast_in_dim.15), channel_id=1, replica_groups=mesh['xp'=4,'xh'=2,'yh'=4,'z'=8,'yl'=2,'core'=2] {'xp','xh','yh'}, dimensions={0} | all-to-all | bytes 32768 | tf_op jit(solution)/shard_map/all_to_all | solution.py:15
  158.9 13.2 %all_to_all.35 = f32[32,1,128]{2,1,0:T(1,128)S(1)} all-to-all(f32[32,1,128]{2,1,0:T(1,128)S(1)} %broadcast_in_dim.16), channel_id=1, replica_groups=mesh['xp'=4,'xh'=2,'yh'=4,'z'=8,'yl'=2,'core'=2] {'z','yl','core'}, dimensions={0} | all-to-all | bytes 32768 | tf_op jit(solution)/shard_map/all_to_all | solution.py:15
  172.2 0.6 reduce_max.73
  (9 shorter events, 0.2 us)
Async XLA Ops:
  0.6 45.7 %copy-start.1 = (bf16[576,1152]{1,0:T(8,128)(2,1)S(1)}, bf16[576,1152]{1,0:T(8,128)(2,1)}, u32[]{:S(2)}) copy-start(bf16[576,1152]{1,0:T(8,128)(2,1)} %param.6) | copy-start | bytes 3981316
  0.6 7.7 %collective-permute-start = (bf16[16,576]{1,0:T(8,128)(2,1)}, bf16[16,576]{1,0:T(8,128)(2,1)S(1)}, u32[]{:S(2)}, u32[]{:S(2)}) collective-permute-start(bf16[16,576]{1,0:T(8,128)(2,1)} %param.5), channel_id=1, source_target_pairs={{0,0},{1,897},{129,128},{128,257},{256,256},{257,129},{385,384},{3... | collective-permute-start | bytes 55304 | tf_op jit(solution)/shard_map/ppermute | solution.py:51
  8.3 38.6 %collective-permute-start.1 = (bf16[576,1152]{1,0:T(8,128)(2,1)}, bf16[576,1152]{1,0:T(8,128)(2,1)S(1)}, u32[]{:S(2)}, u32[]{:S(2)}) collective-permute-start(bf16[576,1152]{1,0:T(8,128)(2,1)} %param.6), channel_id=1, source_target_pairs={{0,896},{128,256},{256,128},{384,512},{512,384},{640,768},{768,640... | collective-permute-start | bytes 3981320 | tf_op jit(solution)/shard_map/ppermute | solution.py:53
  12.1 35.5 %collective-permute-start.2 = (bf16[1152,576]{0,1:T(8,128)(2,1)}, bf16[1152,576]{0,1:T(8,128)(2,1)S(1)}, u32[]{:S(2)}, u32[]{:S(2)}) collective-permute-start(bf16[1152,576]{0,1:T(8,128)(2,1)} %param.7), channel_id=1, source_target_pairs={{0,128},{128,0},{1,129},{129,1},{2,130},{130,2},{3,131},{131,3},{4... | collective-permute-start | bytes 3981320 | tf_op jit(solution)/shard_map/ppermute | solution.py:54
  75.6 27.0 %copy-start = (bf16[1152,576]{0,1:T(8,128)(2,1)S(1)}, bf16[1152,576]{0,1:T(8,128)(2,1)}, u32[]{:S(2)}) copy-start(bf16[1152,576]{0,1:T(8,128)(2,1)} %param.7) | copy-start | bytes 3981316
  110.7 31.6 %copy-start.2 = (s32[16,576]{1,0:T(8,128)S(1)}, s32[16,576]{1,0:T(8,128)}, u32[]{:S(2)}) copy-start(s32[16,576]{1,0:T(8,128)} %param.8) | copy-start | bytes 110596
  110.7 31.6 %copy-start.3 = (bf16[16,576]{1,0:T(8,128)(2,1)S(1)}, bf16[16,576]{1,0:T(8,128)(2,1)}, u32[]{:S(2)}) copy-start(bf16[16,576]{1,0:T(8,128)(2,1)} %param.5) | copy-start | bytes 55300
  137.0 5.3 %collective-permute-start.3 = (f32[16,576]{1,0:T(8,128)S(1)}, f32[16,576]{1,0:T(8,128)S(1)}, u32[]{:S(2)}, u32[]{:S(2)}) collective-permute-start(f32[16,576]{1,0:T(8,128)S(1)} %convert_reduce_fusion.1), channel_id=1, source_target_pairs={{0,0},{1,128},{128,1},{129,129},{2,2},{3,130},{130,3},{131,131},{4... | collective-permute-start | bytes 110600 | tf_op jit(solution)/shard_map/ppermute | solution.py:71

commit v7 on v6

--- a/solution.py
+++ b/solution.py
@@ -48,10 +48,9 @@
     for x in range(n):
         moves.append((2 * x + x % 2, 2 * x))
         moves.append((2 * x + 1 - x % 2, 2 * partner(x, n) + 1))
+    up_other = lax.ppermute(up_weight, ("xp", "xh"), [(x, partner(x, n)) for x in range(n)])
+    down_other = lax.ppermute(down_weight, "xh", [(0, 1), (1, 0)])
     chosen = lax.ppermute(tokens, ("xp", "xh", "core"), moves)
-    chosen, up_sent, down_sent = lax.optimization_barrier((chosen, up_weight, down_weight))
-    up_other = lax.ppermute(up_sent, ("xp", "xh"), [(x, partner(x, n)) for x in range(n)])
-    down_other = lax.ppermute(down_sent, "xh", [(0, 1), (1, 0)])
     half = gather(chosen, ("z", "yl"), blocks)
     both = lax.all_gather(half, "core", axis=0, tiled=True)
     near, far = both[: blocks * rows], both[blocks * rows :]

time: 173 us -> 186 us (1.075)
  waiting for transfers between devices: 4.97 us -> 25 us
  blocking collectives: 149 us -> 134 us
  starting transfers between devices: 13 us -> 19.2 us
    ppermute x1, waiting for transfers between devices: 2.22 us -> 23.9 us  [body(): chosen = lax.ppermute(tokens, ('xp', 'xh', 'core'), moves)]
    all_to_all x6, blocking collectives: 140 us -> 125 us  [exchange(): return lax.all_to_all(blocks, axes, split_axis=0, concat_axis=0, tiled=True)]
    ppermute x1, starting transfers between devices: 1.92 us -> 7.58 us  [body(): lax.ppermute(mlp_out, ('xh', 'core'), [(0, 0), (1, 2), (2, 1), (3, 3)])]
where the time goes in v7:
time: 186 us; the launch traced here: 185 us
  blocking collectives  134 us (72%)
  waiting for transfers between devices  25 us (13%)
  starting transfers between devices  19.2 us (10%)
  matrix products  4.01 us (2%)
    all_to_all x6, blocking collectives, exchange(): return lax.all_to_all(blocks, axes, split_axis=0, concat_axis=0, tiled=True)  125 us
    ppermute x1, waiting for transfers between devices, body(): chosen = lax.ppermute(tokens, ('xp', 'xh', 'core'), moves)  23.9 us
    ppermute x1, starting transfers between devices, body(): lax.ppermute(mlp_out, ('xh', 'core'), [(0, 0), (1, 2), (2, 1), (3, 3)])  7.58 us
    all_gather x1, blocking collectives, body(): lax.all_gather(jnp.where(same, theirs, mine).astype(jnp.bfloat16), 'core'...  6.66 us
    ppermute x1, starting transfers between devices, body(): lax.ppermute(up_weight, ('xp', 'xh'), [(x, partner(x, n)) for x in range(...  5.46 us
    ppermute x1, starting transfers between devices, body(): chosen = lax.ppermute(tokens, ('xp', 'xh', 'core'), moves)  4.21 us
  transfers between devices with their start and end apart: 4, of which 2 were waited for; matrix products, arithmetic and copies ran while one was open for 1% of the time, Pallas kernels for 0%

profile of v7, /device:TPU:1, one launch (start us, length us, event | category | flops | bytes accessed | tf_op | source)
XLA Modules:
  0.0 185.4 jit_solution(11230544327901509825)
XLA Ops:
  0.6 0.0 copy-start.1
  0.6 5.5 %collective-permute-start.1 = (bf16[576,1152]{1,0:T(8,128)(2,1)}, bf16[576,1152]{1,0:T(8,128)(2,1)S(1)}, u32[]{:S(2)}, u32[]{:S(2)}) collective-permute-start(bf16[576,1152]{1,0:T(8,128)(2,1)} %param.6), channel_id=1, source_target_pairs={{0,896},{128,256},{256,128},{384,512},{512,384},{640,768},{768,640... | collective-permute-start | bytes 3981320 | tf_op jit(solution)/shard_map/ppermute | solution.py:51
  6.1 1.9 %collective-permute-start.2 = (bf16[1152,576]{0,1:T(8,128)(2,1)}, bf16[1152,576]{0,1:T(8,128)(2,1)}, u32[]{:S(2)}, u32[]{:S(2)}) collective-permute-start(bf16[1152,576]{0,1:T(8,128)(2,1)} %param.7), channel_id=1, source_target_pairs={{0,128},{128,0},{1,129},{129,1},{2,130},{130,2},{3,131},{131,3},{4... | collective-permute-start | bytes 3981320 | tf_op jit(solution)/shard_map/ppermute | solution.py:52
  8.0 4.2 %collective-permute-start = (bf16[16,576]{1,0:T(8,128)(2,1)}, bf16[16,576]{1,0:T(8,128)(2,1)S(1)}, u32[]{:S(2)}, u32[]{:S(2)}) collective-permute-start(bf16[16,576]{1,0:T(8,128)(2,1)} %param.5), channel_id=1, source_target_pairs={{0,0},{1,897},{129,128},{128,257},{256,256},{257,129},{385,384},{3... | collective-permute-start | bytes 55304 | tf_op jit(solution)/shard_map/ppermute | solution.py:53
  12.3 23.9 %collective-permute-done = bf16[16,576]{1,0:T(8,128)(2,1)S(1)} collective-permute-done((bf16[16,576]{1,0:T(8,128)(2,1)}, bf16[16,576]{1,0:T(8,128)(2,1)S(1)}, u32[]{:S(2)}, u32[]{:S(2)}) %collective-permute-start) | collective-permute-done | bytes 18464 | tf_op jit(solution)/shard_map/ppermute | solution.py:53
  36.2 26.5 %all_to_all.30 = bf16[16,16,576]{2,1,0:T(8,128)(2,1)S(1)} all-to-all(bf16[16,16,576]{2,1,0:T(8,128)(2,1)S(1)} %broadcast_in_dim.13), channel_id=1, replica_groups=mesh['xp'=4,'xh'=2,'yh'=4,'z'=8,'yl'=2,'core'=2] {'z','yl'}, dimensions={0} | all-to-all | bytes 589824 | tf_op jit(solution)/shard_map/all_to_all | solution.py:15
  62.8 2.3 %all_gather.9 = bf16[512,576]{1,0:T(8,128)(2,1)S(1)} all-gather(bf16[256,576]{1,0:T(8,128)(2,1)S(1)} %bitcast.18), channel_id=1, replica_groups=mesh['xp'=4,'xh'=2,'yh'=4,'z'=8,'yl'=2,'core'=2] {'core'}, dimensions={0}, use_global_device_ids=true | all-gather | bytes 884736 | tf_op jit(solution)/shard_map/all_gather | solution.py:55
  65.0 0.0 copy-done.1
  65.0 0.6 fusion.4
  65.7 0.0 collective-permute-done.1
  65.7 0.6 fusion.1
  66.3 0.0 collective-permute-done.2
  66.3 30.4 %all_to_all.31 = f16[16,16,1152]{2,1,0:T(8,128)(2,1)S(1)} all-to-all(f16[16,16,1152]{2,1,0:T(8,128)(2,1)S(1)} %bitcast.17), channel_id=1, replica_groups=mesh['xp'=4,'xh'=2,'yh'=4,'z'=8,'yl'=2,'core'=2] {'xp','yh'}, dimensions={0} | all-to-all | bytes 1179648 | tf_op jit(solution)/shard_map/all_to_all | solution.py:15
  96.7 0.0 copy-start
  96.7 0.1 convert_reduce_fusion
  96.9 27.1 %all_to_all.32 = bf16[16,16,1152]{2,1,0:T(8,128)(2,1)S(1)} all-to-all(bf16[16,16,1152]{2,1,0:T(8,128)(2,1)S(1)} %broadcast_in_dim.14), channel_id=1, replica_groups=mesh['xp'=4,'xh'=2,'yh'=4,'z'=8,'yl'=2,'core'=2] {'xp','yh'}, dimensions={0} | all-to-all | bytes 1179648 | tf_op jit(solution)/shard_map/all_to_all | solution.py:15
  124.0 0.0 copy-done
  124.0 0.7 fusion.7
  124.7 2.0 %select_convert_fusion = (bf16[256,576]{1,0:T(8,128)(2,1)S(1)}, f32[256,576]{1,0:T(8,128)S(1)}) fusion(f32[256,576]{1,0:T(8,128)S(1)} %fusion.7, pred[]{:T(512)S(6)} %eq.7, bf16[256,1152]{1,0:T(8,128)(2,1)S(1)} %bitcast.16, bf16[1152,576]{0,1:T(8,128)(2,1)} %collective-permute-done.2), kind=kOutput, calls=%fused_computation.7 | convolution fusion | flops 339886080 | bytes 3391489 | tf_op jit(solution)/shard_map/dot_general | solution.py:65
  126.8 6.7 %all-gather = bf16[512,576]{1,0:T(8,128)(2,1)S(1)} all-gather(bf16[256,576]{1,0:T(8,128)(2,1)S(1)} %get-tuple-element.18), channel_id=2, replica_groups=mesh['xp'=4,'xh'=2,'yh'=4,'z'=8,'yl'=2,'core'=2] {'core'}, dimensions={0}, use_global_device_ids=true | all-gather | bytes 884736 | tf_op jit(solution)/shard_map/all_gather | solution.py:66
  133.4 0.0 copy-start.2
  133.4 0.0 copy-start.3
  133.4 0.2 fusion.2
  133.6 14.0 %all_to_all.33 = bf16[16,16,576]{2,1,0:T(8,128)(2,1)S(1)} all-to-all(bf16[16,16,576]{2,1,0:T(8,128)(2,1)S(1)} %bitcast.19), channel_id=1, replica_groups=mesh['xp'=4,'xh'=2,'yh'=4,'z'=8,'yl'=2,'core'=2] {'z','yl'}, dimensions={0} | all-to-all | bytes 589824 | tf_op jit(solution)/shard_map/all_to_all | solution.py:15
  147.6 0.1 convert_reduce_fusion.1
  147.6 7.6 %collective-permute-start.3 = (f32[16,576]{1,0:T(8,128)S(1)}, f32[16,576]{1,0:T(8,128)S(1)}, u32[]{:S(2)}, u32[]{:S(2)}) collective-permute-start(f32[16,576]{1,0:T(8,128)S(1)} %convert_reduce_fusion.1), channel_id=1, source_target_pairs={{0,0},{1,128},{128,1},{129,129},{2,2},{3,130},{130,3},{131,131},{4... | collective-permute-start | bytes 110600 | tf_op jit(solution)/shard_map/ppermute | solution.py:70
  155.9 1.0 collective-permute-done.3
  156.9 0.0 copy-done.2
  156.9 0.0 copy-done.3
  156.9 0.6 fusion.6
  157.6 14.0 %all_to_all.34 = f32[32,1,128]{2,1,0:T(1,128)S(1)} all-to-all(f32[32,1,128]{2,1,0:T(1,128)S(1)} %broadcast_in_dim.15), channel_id=1, replica_groups=mesh['xp'=4,'xh'=2,'yh'=4,'z'=8,'yl'=2,'core'=2] {'xp','xh','yh'}, dimensions={0} | all-to-all | bytes 32768 | tf_op jit(solution)/shard_map/all_to_all | solution.py:15
  171.7 13.1 %all_to_all.35 = f32[32,1,128]{2,1,0:T(1,128)S(1)} all-to-all(f32[32,1,128]{2,1,0:T(1,128)S(1)} %broadcast_in_dim.16), channel_id=1, replica_groups=mesh['xp'=4,'xh'=2,'yh'=4,'z'=8,'yl'=2,'core'=2] {'z','yl','core'}, dimensions={0} | all-to-all | bytes 32768 | tf_op jit(solution)/shard_map/all_to_all | solution.py:15
  184.8 0.6 reduce_max.73
  (9 shorter events, 0.2 us)
Async XLA Ops:
  0.6 64.4 %copy-start.1 = (bf16[576,1152]{1,0:T(8,128)(2,1)S(1)}, bf16[576,1152]{1,0:T(8,128)(2,1)}, u32[]{:S(2)}) copy-start(bf16[576,1152]{1,0:T(8,128)(2,1)} %param.6) | copy-start | bytes 3981316
  0.6 65.0 %collective-permute-start.1 = (bf16[576,1152]{1,0:T(8,128)(2,1)}, bf16[576,1152]{1,0:T(8,128)(2,1)S(1)}, u32[]{:S(2)}, u32[]{:S(2)}) collective-permute-start(bf16[576,1152]{1,0:T(8,128)(2,1)} %param.6), channel_id=1, source_target_pairs={{0,896},{128,256},{256,128},{384,512},{512,384},{640,768},{768,640... | collective-permute-start | bytes 3981320 | tf_op jit(solution)/shard_map/ppermute | solution.py:51
  6.1 60.2 %collective-permute-start.2 = (bf16[1152,576]{0,1:T(8,128)(2,1)}, bf16[1152,576]{0,1:T(8,128)(2,1)}, u32[]{:S(2)}, u32[]{:S(2)}) collective-permute-start(bf16[1152,576]{0,1:T(8,128)(2,1)} %param.7), channel_id=1, source_target_pairs={{0,128},{128,0},{1,129},{129,1},{2,130},{130,2},{3,131},{131,3},{4... | collective-permute-start | bytes 3981320 | tf_op jit(solution)/shard_map/ppermute | solution.py:52
  8.0 28.2 %collective-permute-start = (bf16[16,576]{1,0:T(8,128)(2,1)}, bf16[16,576]{1,0:T(8,128)(2,1)S(1)}, u32[]{:S(2)}, u32[]{:S(2)}) collective-permute-start(bf16[16,576]{1,0:T(8,128)(2,1)} %param.5), channel_id=1, source_target_pairs={{0,0},{1,897},{129,128},{128,257},{256,256},{257,129},{385,384},{3... | collective-permute-start | bytes 55304 | tf_op jit(solution)/shard_map/ppermute | solution.py:53
  96.7 27.3 %copy-start = (bf16[1152,576]{0,1:T(8,128)(2,1)S(1)}, bf16[1152,576]{0,1:T(8,128)(2,1)}, u32[]{:S(2)}) copy-start(bf16[1152,576]{0,1:T(8,128)(2,1)} %param.7) | copy-start | bytes 3981316
  133.4 23.5 %copy-start.2 = (s32[16,576]{1,0:T(8,128)S(1)}, s32[16,576]{1,0:T(8,128)}, u32[]{:S(2)}) copy-start(s32[16,576]{1,0:T(8,128)} %param.8) | copy-start | bytes 110596
  133.4 23.5 %copy-start.3 = (bf16[16,576]{1,0:T(8,128)(2,1)S(1)}, bf16[16,576]{1,0:T(8,128)(2,1)}, u32[]{:S(2)}) copy-start(bf16[16,576]{1,0:T(8,128)(2,1)} %param.5) | copy-start | bytes 55300
  147.6 9.3 %collective-permute-start.3 = (f32[16,576]{1,0:T(8,128)S(1)}, f32[16,576]{1,0:T(8,128)S(1)}, u32[]{:S(2)}, u32[]{:S(2)}) collective-permute-start(f32[16,576]{1,0:T(8,128)S(1)} %convert_reduce_fusion.1), channel_id=1, source_target_pairs={{0,0},{1,128},{128,1},{129,129},{2,2},{3,130},{130,3},{131,131},{4... | collective-permute-start | bytes 110600 | tf_op jit(solution)/shard_map/ppermute | solution.py:70

commit v8 on v7

--- a/solution.py
+++ b/solution.py
@@ -7,7 +7,7 @@
 DP = ("xp", "xh", "yh")
 TENSOR = ("z", "yl", "core")
 LIKE = ("xp", "yh")
-LIFT = 64.0
+LIFT = 128.0
 ROW_MAJOR = Layout(major_to_minor=(0, 1))
 
 
@@ -33,32 +33,19 @@
     return largest[None]
 
 
-def partner(x, n):
-    return (x + 1) % n if x % 2 else (x - 1) % n
-
-
 def body(tokens, up_weight, down_weight, keep_bits, prior_scale):
     rows, width = tokens.shape
     shards = up_weight.shape[1]
-    n = 2 * lax.axis_size("xp")
     blocks = lax.axis_size("z") * lax.axis_size("yl")
     core = lax.axis_index("core")
     first, same, tokens = lax.optimization_barrier((core == 0, core == lax.axis_index("xh"), tokens))
-    moves = []
-    for x in range(n):
-        moves.append((2 * x + x % 2, 2 * x))
-        moves.append((2 * x + 1 - x % 2, 2 * partner(x, n) + 1))
-    up_other = lax.ppermute(up_weight, ("xp", "xh"), [(x, partner(x, n)) for x in range(n)])
     down_other = lax.ppermute(down_weight, "xh", [(0, 1), (1, 0)])
-    chosen = lax.ppermute(tokens, ("xp", "xh", "core"), moves)
-    half = gather(chosen, ("z", "yl"), blocks)
-    both = lax.all_gather(half, "core", axis=0, tiled=True)
-    near, far = both[: blocks * rows], both[blocks * rows :]
-    hidden_part = jnp.dot(near, up_weight, preferred_element_type=jnp.float32)
-    hidden_part = hidden_part + jnp.dot(far, up_other, preferred_element_type=jnp.float32)
-    hidden_part = (hidden_part * LIFT).astype(jnp.float16).reshape(blocks, rows, shards)
+    half = gather(tokens, ("z", "yl"), blocks)
+    gathered = lax.all_gather(half, "core", axis=0, tiled=True)
+    hidden_part = jnp.dot(gathered, up_weight, preferred_element_type=jnp.float32)
+    hidden_part = (hidden_part * LIFT).astype(jnp.float16).reshape(2 * blocks, rows, shards)
     hidden_part, down_other = lax.optimization_barrier((hidden_part, down_other))
-    hidden = jnp.sum(exchange(hidden_part, LIKE).astype(jnp.float32), axis=0) * (1.0 / LIFT)
+    hidden = jnp.sum(exchange(hidden_part, ("xh",) + LIKE).astype(jnp.float32), axis=0) * (1.0 / LIFT)
     positive = jnp.maximum(hidden, 0.0)
     active = gather((positive * positive).astype(jnp.bfloat16), LIKE, blocks)
     mine = with_layout_constraint(jnp.dot(active, down_weight, preferred_element_type=jnp.float32), ROW_MAJOR)
@@ -70,7 +57,7 @@
     mlp_out = lax.ppermute(mlp_out, ("xh", "core"), [(0, 0), (1, 2), (2, 1), (3, 3)])
     combined = tokens.astype(jnp.float32) + keep_bits.astype(jnp.float32) * mlp_out / 0.9
     largest = lane_maxima(jnp.abs(combined))
-    amax = jnp.max(max_over(max_over(largest, DP, n * lax.axis_size("yh")), TENSOR, 2 * blocks)).reshape(1)
+    amax = jnp.max(max_over(max_over(largest, DP, 2 * blocks), TENSOR, 2 * blocks)).reshape(1)
     scaled = jnp.clip(combined * prior_scale[0], -448.0, 448.0).astype(jnp.bfloat16)
     return (scaled, amax)
 

time: 186 us -> 176 us (0.946)
  blocking collectives: 134 us -> 160 us
  waiting for transfers between devices: 25 us -> 2.75 us
  starting transfers between devices: 19.2 us -> 6 us
    all_to_all x6, blocking collectives: 125 us -> 150 us  [exchange(): return lax.all_to_all(blocks, axes, split_axis=0, concat_axis=0, tiled=True)]
    ppermute x2 -> x0, waiting for transfers between devices: 24 us -> none  [the longest x1 23.9 us: body(): chosen = lax.ppermute(tokens, ('xp', 'xh', 'core'), moves)]
    ppermute x2 -> x0, starting transfers between devices: 9.67 us -> none  [the longest x1 5.46 us: body(): lax.ppermute(up_weight, ('xp', 'xh'), [(x, partner(x, n)) for x in range(...]
    ppermute x1, starting transfers between devices: 7.58 us -> 1.92 us  [body(): lax.ppermute(mlp_out, ('xh', 'core'), [(0, 0), (1, 2), (2, 1), (3, 3)])]
    ppermute x1, starting transfers between devices: 1.92 us -> 4.08 us  [body(): down_other = lax.ppermute(down_weight, 'xh', [(0, 1), (1, 0)])]
    all_gather x1, blocking collectives: 2.26 us -> 4.34 us  [body(): gathered = lax.all_gather(half, 'core', axis=0, tiled=True)]
  transfers between devices with their start and end apart: 4 -> 2, of which waited for: 2 -> 1; matrix products, arithmetic and copies ran while one was open for 1% -> 1% of each run, Pallas kernels for 0% -> 0%
where the time goes in v8:
time: 176 us; the launch traced here: 175 us
  blocking collectives  160 us (91%)
  starting transfers between devices  6 us (3%)
  waiting for transfers between devices  2.75 us (2%)
  matrix products  2.54 us (1%)
    all_to_all x6, blocking collectives, exchange(): return lax.all_to_all(blocks, axes, split_axis=0, concat_axis=0, tiled=True)  150 us
    all_gather x1, blocking collectives, body(): lax.all_gather(jnp.where(same, theirs, mine).astype(jnp.bfloat16), 'core'...  5.89 us
    all_gather x1, blocking collectives, body(): gathered = lax.all_gather(half, 'core', axis=0, tiled=True)  4.34 us
    ppermute x1, starting transfers between devices, body(): down_other = lax.ppermute(down_weight, 'xh', [(0, 1), (1, 0)])  4.08 us
  transfers between devices with their start and end apart: 2, of which 1 were waited for; matrix products, arithmetic and copies ran while one was open for 1% of the time, Pallas kernels for 0%

profile of v8, /device:TPU:1, one launch (start us, length us, event | category | flops | bytes accessed | tf_op | source)
XLA Modules:
  0.0 175.3 jit_solution(5544766904517066205)
XLA Ops:
  0.6 0.0 copy-start
  0.6 4.1 %collective-permute-start = (bf16[1152,576]{0,1:T(8,128)(2,1)}, bf16[1152,576]{0,1:T(8,128)(2,1)S(1)}, u32[]{:S(2)}, u32[]{:S(2)}) collective-permute-start(bf16[1152,576]{0,1:T(8,128)(2,1)} %param.7), channel_id=1, source_target_pairs={{0,128},{128,0},{1,129},{129,1},{2,130},{130,2},{3,131},{131,3},{4... | collective-permute-start | bytes 3981320 | tf_op jit(solution)/shard_map/ppermute | solution.py:42
  4.7 0.8 broadcast_in_dim.13
  5.5 28.7 %all_to_all.30 = bf16[16,16,576]{2,1,0:T(8,128)(2,1)S(1)} all-to-all(bf16[16,16,576]{2,1,0:T(8,128)(2,1)S(1)} %broadcast_in_dim.13), channel_id=1, replica_groups=mesh['xp'=4,'xh'=2,'yh'=4,'z'=8,'yl'=2,'core'=2] {'z','yl'}, dimensions={0} | all-to-all | bytes 589824 | tf_op jit(solution)/shard_map/all_to_all | solution.py:15
  34.2 4.3 %all_gather.9 = bf16[512,576]{1,0:T(8,128)(2,1)S(1)} all-gather(bf16[256,576]{1,0:T(8,128)(2,1)S(1)} %bitcast.17), channel_id=1, replica_groups=mesh['xp'=4,'xh'=2,'yh'=4,'z'=8,'yl'=2,'core'=2] {'core'}, dimensions={0}, use_global_device_ids=true | all-gather | bytes 884736 | tf_op jit(solution)/shard_map/all_gather | solution.py:44
  38.5 0.0 copy-done
  38.5 1.2 fusion
  39.7 0.0 collective-permute-done
  39.7 43.6 %all_to_all.31 = f16[32,16,1152]{2,1,0:T(8,128)(2,1)S(1)} all-to-all(f16[32,16,1152]{2,1,0:T(8,128)(2,1)S(1)} %bitcast.19), channel_id=1, replica_groups=mesh['xp'=4,'xh'=2,'yh'=4,'z'=8,'yl'=2,'core'=2] {'xh','xp','yh'}, dimensions={0} | all-to-all | bytes 2359296 | tf_op jit(solution)/shard_map/all_to_all | solution.py:15
  83.3 0.0 copy-start.1
  83.3 0.2 convert_reduce_fusion
  83.5 23.6 %all_to_all.32 = bf16[16,16,1152]{2,1,0:T(8,128)(2,1)S(1)} all-to-all(bf16[16,16,1152]{2,1,0:T(8,128)(2,1)S(1)} %broadcast_in_dim.14), channel_id=1, replica_groups=mesh['xp'=4,'xh'=2,'yh'=4,'z'=8,'yl'=2,'core'=2] {'xp','yh'}, dimensions={0} | all-to-all | bytes 1179648 | tf_op jit(solution)/shard_map/all_to_all | solution.py:15
  107.1 0.0 copy-done.1
  107.1 0.7 fusion.3
  107.8 0.7 select_convert_fusion
  108.5 5.9 %all-gather = bf16[512,576]{1,0:T(8,128)(2,1)S(1)} all-gather(bf16[256,576]{1,0:T(8,128)(2,1)S(1)} %get-tuple-element.18), channel_id=2, replica_groups=mesh['xp'=4,'xh'=2,'yh'=4,'z'=8,'yl'=2,'core'=2] {'core'}, dimensions={0}, use_global_device_ids=true | all-gather | bytes 884736 | tf_op jit(solution)/shard_map/all_gather | solution.py:53
  114.4 0.0 copy-start.2
  114.4 0.0 copy-start.3
  114.4 0.2 fusion.1
  114.6 25.5 %all_to_all.33 = bf16[16,16,576]{2,1,0:T(8,128)(2,1)S(1)} all-to-all(bf16[16,16,576]{2,1,0:T(8,128)(2,1)S(1)} %bitcast.18), channel_id=1, replica_groups=mesh['xp'=4,'xh'=2,'yh'=4,'z'=8,'yl'=2,'core'=2] {'z','yl'}, dimensions={0} | all-to-all | bytes 589824 | tf_op jit(solution)/shard_map/all_to_all | solution.py:15
  140.0 0.1 convert_reduce_fusion.1
  140.1 1.9 %collective-permute-start.1 = (f32[16,576]{1,0:T(8,128)S(1)}, f32[16,576]{1,0:T(8,128)S(1)}, u32[]{:S(2)}, u32[]{:S(2)}) collective-permute-start(f32[16,576]{1,0:T(8,128)S(1)} %convert_reduce_fusion.1), channel_id=1, source_target_pairs={{0,0},{1,128},{128,1},{129,129},{2,2},{3,130},{130,3},{131,131},{4... | collective-permute-start | bytes 110600 | tf_op jit(solution)/shard_map/ppermute | solution.py:57
  142.7 2.7 %collective-permute-done.1 = f32[16,576]{1,0:T(8,128)S(1)} collective-permute-done((f32[16,576]{1,0:T(8,128)S(1)}, f32[16,576]{1,0:T(8,128)S(1)}, u32[]{:S(2)}, u32[]{:S(2)}) %collective-permute-start.1) | collective-permute-done | bytes 36896 | tf_op jit(solution)/shard_map/ppermute | solution.py:57
  145.4 0.0 copy-done.2
  145.4 0.0 copy-done.3
  145.4 0.6 fusion.2
  146.1 14.7 %all_to_all.34 = f32[32,1,128]{2,1,0:T(1,128)S(1)} all-to-all(f32[32,1,128]{2,1,0:T(1,128)S(1)} %broadcast_in_dim.15), channel_id=1, replica_groups=mesh['xp'=4,'xh'=2,'yh'=4,'z'=8,'yl'=2,'core'=2] {'xp','xh','yh'}, dimensions={0} | all-to-all | bytes 32768 | tf_op jit(solution)/shard_map/all_to_all | solution.py:15
  160.9 13.9 %all_to_all.35 = f32[32,1,128]{2,1,0:T(1,128)S(1)} all-to-all(f32[32,1,128]{2,1,0:T(1,128)S(1)} %broadcast_in_dim.16), channel_id=1, replica_groups=mesh['xp'=4,'xh'=2,'yh'=4,'z'=8,'yl'=2,'core'=2] {'z','yl','core'}, dimensions={0} | all-to-all | bytes 32768 | tf_op jit(solution)/shard_map/all_to_all | solution.py:15
  174.7 0.6 reduce_max.73
  (8 shorter events, 0.1 us)
Async XLA Ops:
  0.6 37.9 %copy-start = (bf16[576,1152]{1,0:T(8,128)(2,1)S(1)}, bf16[576,1152]{1,0:T(8,128)(2,1)}, u32[]{:S(2)}) copy-start(bf16[576,1152]{1,0:T(8,128)(2,1)} %param.6) | copy-start | bytes 3981316
  0.6 39.1 %collective-permute-start = (bf16[1152,576]{0,1:T(8,128)(2,1)}, bf16[1152,576]{0,1:T(8,128)(2,1)S(1)}, u32[]{:S(2)}, u32[]{:S(2)}) collective-permute-start(bf16[1152,576]{0,1:T(8,128)(2,1)} %param.7), channel_id=1, source_target_pairs={{0,128},{128,0},{1,129},{129,1},{2,130},{130,2},{3,131},{131,3},{4... | collective-permute-start | bytes 3981320 | tf_op jit(solution)/shard_map/ppermute | solution.py:42
  83.3 23.8 %copy-start.1 = (bf16[1152,576]{0,1:T(8,128)(2,1)S(1)}, bf16[1152,576]{0,1:T(8,128)(2,1)}, u32[]{:S(2)}) copy-start(bf16[1152,576]{0,1:T(8,128)(2,1)} %param.7) | copy-start | bytes 3981316
  114.4 31.0 %copy-start.2 = (bf16[16,576]{1,0:T(8,128)(2,1)S(1)}, bf16[16,576]{1,0:T(8,128)(2,1)}, u32[]{:S(2)}) copy-start(bf16[16,576]{1,0:T(8,128)(2,1)} %param.5) | copy-start | bytes 55300
  114.4 31.0 %copy-start.3 = (s32[16,576]{1,0:T(8,128)S(1)}, s32[16,576]{1,0:T(8,128)}, u32[]{:S(2)}) copy-start(s32[16,576]{1,0:T(8,128)} %param.8) | copy-start | bytes 110596
  140.1 5.3 %collective-permute-start.1 = (f32[16,576]{1,0:T(8,128)S(1)}, f32[16,576]{1,0:T(8,128)S(1)}, u32[]{:S(2)}, u32[]{:S(2)}) collective-permute-start(f32[16,576]{1,0:T(8,128)S(1)} %convert_reduce_fusion.1), channel_id=1, source_target_pairs={{0,0},{1,128},{128,1},{129,129},{2,2},{3,130},{130,3},{131,131},{4... | collective-permute-start | bytes 110600 | tf_op jit(solution)/shard_map/ppermute | solution.py:57
